TPU v7x, 32 devices: a whole 2x2x4 slice. The times are simulated.
32 devices in a mesh: groups: 2 (over x), paths: 2 (over core), feats: 8 (over z, y).
Axes of the slice: x: 2, y: 2, z: 4, core: 2. Of those that a mesh axis runs over, the one named last changes fastest.
Arguments:
- factors: int32 [4096, 128], P(('groups', 'paths')), parts along dimension 0, may hold values from -8 to 8
- frequency: int32 [128, 65536], P(None, 'feats'), may hold values from -48 to 48
- phases: int32 [65536], P('feats'), may hold values from 0 to 1023
- amplitude: float32 [65536], P('feats'), as said below
- targets: float32 [32, 4096], P(None, ('groups', 'paths')), parts along dimension 1, may hold values from -6 to 6
- coeffs_init: float32 [32, 131072], P(None, ('groups', 'feats')), parts along dimension 1, may hold values from -6 to 6
Outputs:
- coeffs: float32 [32, 131072], P(None, ('groups', 'feats')), parts along dimension 1
- predicted: float32 [32, 4096], P(None, ('groups', 'paths')), parts along dimension 1
There are 2 independent parts, one for each index of `groups`. A program takes and returns all parts, laid end to end along the dimension named above; an argument that names none is the same for every part. Nothing has to cross between parts.
Inputs may be any that keep to these rules, and one draw needn't show every extreme that they name: `amplitude`: positive feature weights.
All inputs are finite; a program needn't handle non-finite values.
Results may differ from a plain program's by a relative error of at most 0.00026.
Values sent between devices are 32-bit elements; how exact they have to be, the bound alone decides.
No kernel may reach another device: no remote copies, remote signals or barrier semaphores. Data moves between devices by JAX's collectives and lax.ppermute only.
A program may use at most 128 MiB of HBM per device.

v0:
```python
import functools
import math

import jax
import jax.numpy as jnp
import numpy as np
from jax import lax
from jax.experimental import pallas as pl
from jax.experimental.pallas import tpu as pltpu
from jax.sharding import PartitionSpec as P

ITERS = 3

huber_cap = 1.0
step_rate = 0.2
momentum = 0.9
epsilon = 1e-06

f32 = jnp.float32
bf16 = jnp.bfloat16
f8 = jnp.float8_e4m3fn
NN = (((1,), (0,)), ((), ()))
NT = (((1,), (1,)), ((), ()))
TURN = 0.0025 / (2.0 * math.pi)


def fit_half_angle():
    rest = np.cos(np.linspace(0, np.pi, 4001)) * 0.5
    target = np.cos(np.pi * rest)
    basis = np.stack([rest ** (2 * i) for i in range(4)], 1)
    weight = np.abs(target) + 1e-3
    return np.linalg.lstsq(basis * weight[:, None], target * weight, rcond=None)[0]


HALF = fit_half_angle()
TOP = float(2.0 * HALF[-1] ** 2)
SERIES = [float(term / HALF[-1]) for term in HALF]
LOW = 2.0**15
CLIP = 256.0
GRANT = 20


def split(values):
    high = values.astype(bf16)
    return high, (values - high.astype(f32)).astype(bf16)


def cosine(turns):
    rest = turns - jnp.round(turns)
    square = rest * rest
    series = square + SERIES[2]
    series = series * square + SERIES[1]
    series = series * square + SERIES[0]
    return series * series - 1.0 / TOP


def divisor(size, most):
    while size % most:
        most //= 2
    return most


def padded(factors, width):
    rows, risks = factors.shape
    ones = (lax.broadcasted_iota(jnp.int32, (rows, width - risks), 1) < 3).astype(f32)
    return jnp.concatenate([factors.astype(f32).astype(bf16), ones.astype(bf16)], 1)


def prepare_kernel(
    own_ref, freq_ref, phase_ref, amp_ref, coeffs_ref, factor_out, freq_out, start_out, amp_out,
    own_buf, freq_buf, phase_buf, amp_buf, coeffs_buf, whole_sem, freq_sem,
):
    risks = own_ref.shape[1]
    count = coeffs_ref.shape[0]
    steps, _, cols = freq_buf.shape
    extra = freq_out.shape[0] - risks
    first = lax.axis_index("paths") * cols * steps

    def fetch(index):
        source = pl.ds(pl.multiple_of(first + index * cols, cols), cols)
        return pltpu.make_async_copy(freq_ref.at[:, source], freq_buf.at[index], freq_sem.at[index])

    mine = pl.ds(pl.multiple_of(first, cols), cols * steps)
    wholes = [
        pltpu.make_async_copy(source, target, whole_sem.at[number])
        for number, (source, target) in enumerate(
            (
                (phase_ref.at[:, mine], phase_buf),
                (amp_ref.at[:, mine], amp_buf),
                (coeffs_ref.at[:, mine], coeffs_buf),
                (own_ref, own_buf),
            )
        )
    ]
    for copy in wholes:
        copy.start()
    for index in range(steps):
        fetch(index).start()
    for copy in wholes:
        copy.wait()
    factor_out[...] = padded(own_buf[...], factor_out.shape[1])
    row = lax.broadcasted_iota(jnp.int32, (extra, cols), 0)
    for index in range(steps):
        span = pl.ds(index * cols, cols)
        phase = phase_buf[:, span].astype(f32) * (1.0 / (1024.0 * TURN))
        piece_high = phase.astype(bf16).astype(f32)
        piece_middle = (phase - piece_high).astype(bf16).astype(f32)
        piece_low = phase - piece_high - piece_middle
        pieces = jnp.where(row == 0, piece_high, jnp.where(row == 1, piece_middle, jnp.where(row == 2, piece_low, 0.0)))
        freq_out[risks:, span] = pieces.astype(bf16)
        amp = amp_buf[:, span] * TOP
        amp_out[:, span] = amp
        start_high, start_low = split(coeffs_buf[:, span] * amp)
        start_out[:count, span] = start_high
        start_out[count:, span] = start_low
    for index in range(steps):
        fetch(index).wait()
        freq_out[:risks, pl.ds(index * cols, cols)] = freq_buf[index].astype(f32).astype(bf16)


def build_kernel(
    own_ref, other_ref, freq_ref, start_ref, blank_high, blank_low, image_own, image_other, high_ref, low_ref, other_buf
):
    paths, width = high_ref.shape
    half = paths // 2
    cols = divisor(width, 1024)
    rows = divisor(half, 512)
    count = start_ref.shape[0] // 2
    other_buf[...] = padded(other_ref[...], other_buf.shape[1])

    image_own[...] = jnp.zeros_like(image_own)
    image_other[...] = jnp.zeros_like(image_other)

    def block(index, carry):
        span = pl.ds(pl.multiple_of(index * cols, cols), cols)
        freq, start = freq_ref[:, span], start_ref[:, span]

        def sums_of(part):
            factor_ref = own_ref if part * rows < half else other_buf
            factors = factor_ref[pl.ds(part * rows % half, rows), :]
            return lax.dot_general(factors, freq, NN, preferred_element_type=f32)

        def add_image(part, high, low):
            main = lax.dot_general(start, high, NT, preferred_element_type=f32)
            rest = lax.dot_general(low, start[:count], NT, preferred_element_type=f32)
            image_ref = image_own if part * rows < half else image_other
            image_ref[:, pl.ds(part * rows % half, rows)] += main[:count] + main[count:] + rest.T

        parts = paths // rows
        summed = sums_of(0)
        before = None
        for part in range(parts):
            summed_after = sums_of(part + 1) if part + 1 < parts else None
            place = pl.ds(part * rows, rows)
            values = cosine(summed * TURN)
            high = values.astype(bf16)
            rest = values - high.astype(f32)
            high_ref[place, span] = high
            low_ref[place, span] = (rest * LOW).astype(f8)
            if before is not None:
                add_image(*before)
            before = part, high, rest.astype(bf16)
            summed = summed_after
        add_image(*before)
        return carry

    lax.fori_loop(0, width // cols, block, 0)


def gradient_of(clipped, high_ref, low_ref, place, span):
    count = clipped.shape[0]
    pair = jnp.concatenate(split(clipped), 0)
    main = lax.dot_general(pair, high_ref[place, span], NN, preferred_element_type=f32)
    coarse = (clipped * CLIP).astype(f8)
    rest = lax.dot_general(coarse, low_ref[place, span], NN, preferred_element_type=f32)
    return main[:count] + main[count:] + rest * (1.0 / (CLIP * LOW))


def image_of(pair_ref, coarse_ref, level, high_ref, low_ref, place, image_ref):
    count = pair_ref.shape[0] // 2
    main = lax.dot_general(pair_ref[...], high_ref[place, :], NT, preferred_element_type=f32)
    rest = lax.dot_general(coarse_ref[...], low_ref[place, :], NT, preferred_element_type=f32)
    image = main[:count] + main[count:] + rest * (level * (1.0 / LOW))
    for tile in range(image.shape[1] // 128):
        image_ref[pl.ds(tile * count, count), :] = image[:, tile * 128 : tile * 128 + 128]


def own_kernel(clipped_ref, high_ref, low_ref, partial_out):
    paths, width = high_ref.shape
    cols = divisor(width, 1024)
    for index in range(width // cols):
        span = pl.ds(index * cols, cols)
        partial_out[:, span] = gradient_of(clipped_ref[...], high_ref, low_ref, pl.ds(0, paths // 2), span)


def rest_kernel(
    clipped_ref, high_ref, low_ref, partial_ref, amp_ref, grad_out, pair_out, coarse_out, image_out, notes_out
):
    paths, width = high_ref.shape
    half = paths // 2
    count = clipped_ref.shape[0]
    cols = divisor(width, 1024)
    squares = jnp.zeros((8, 128), f32)
    largest = jnp.zeros((count, 128), f32)
    for index in range(width // cols):
        span = pl.ds(index * cols, cols)
        share = gradient_of(clipped_ref[...], high_ref, low_ref, pl.ds(half, half), span)
        amp = amp_ref[:, span]
        grad = (partial_ref[:, span] + share) * amp
        grad_out[:, span] = grad
        pushed = grad * amp
        high, low = split(pushed)
        pair_out[:count, span] = high
        pair_out[count:, span] = low
        for lane in range(0, cols, 128):
            largest = jnp.maximum(largest, jnp.abs(pushed[:, lane : lane + 128]))
            for row in range(0, count, 8):
                tile = grad[row : row + 8, lane : lane + 128]
                squares = squares + tile * tile
    level = jnp.maximum(jnp.max(largest, axis=1, keepdims=True), 1e-30) * (1.0 / 240.0)
    for index in range(width // cols):
        span = pl.ds(index * cols, cols)
        coarse_out[:, span] = (pair_out[:count, span].astype(f32) * (1.0 / level)).astype(f8)
    image_of(pair_out, coarse_out, level, high_ref, low_ref, pl.ds(half, half), image_out)
    image_out[pl.ds(count * half // 128, 8), :] = squares
    notes_out[:8, :] = squares
    notes_out[8:, :] = jnp.broadcast_to(level, (count, 128))


def image_kernel(pair_ref, coarse_ref, notes_ref, high_ref, low_ref, image_out):
    half = high_ref.shape[0] // 2
    image_of(pair_ref, coarse_ref, notes_ref[8:, :1], high_ref, low_ref, pl.ds(0, half), image_out)
    image_out[pl.ds(pair_ref.shape[0] // 2 * half // 128, 8), :] = notes_ref[:8, :]


def start_kernel(own_ref, other_ref, front_out, back_out):
    count, half = own_ref.shape
    tiles = half // 128
    for tile in range(tiles):
        out = front_out if tile < tiles // 2 else back_out
        span = pl.ds(tile * 128, 128)
        out[pl.ds(tile % (tiles // 2) * count, count), :] = own_ref[:, span] + other_ref[:, span]


def join_kernel(own_ref, other_ref, front_out, back_out):
    middle, end = back_out.shape[0], 2 * back_out.shape[0]
    front_out[:middle, :] = own_ref[:middle, :] + other_ref[:middle, :]
    front_out[middle:, :] = own_ref[end:, :] + other_ref[end:, :]
    back_out[...] = own_ref[middle:end, :] + other_ref[middle:end, :]


def add_kernel(one_ref, other_ref, sum_ref):
    sum_ref[...] = one_ref[...] + other_ref[...]


def places(targets_ref, front, back):
    count, half = targets_ref.shape
    tiles = half // 128
    for tile in range(tiles):
        refs = front if tile < tiles // 2 else back
        yield pl.ds(tile * 128, 128), refs, pl.ds(tile % (tiles // 2) * count, count)


def open_kernel(front, front_last, back, back_last, targets_ref, clipped_out, predicted_out):
    for span, (one, other), rows in places(targets_ref, (front, front_last), (back, back_last)):
        predicted = one[rows, :] + other[rows, :]
        predicted_out[:, span] = predicted
        clipped_out[:, span] = jnp.clip(predicted - targets_ref[:, span], -huber_cap, huber_cap)


def inverse_of(entries, front, front_last, back):
    end = pl.ds(back.shape[0], 8)
    total = jnp.sum(front[end, :] + front_last[end, :], axis=(0, 1), keepdims=True)
    return 1.0 / jnp.sqrt(total / entries + epsilon)


def step_kernel(entries, front, front_last, back, back_last, targets_ref, predicted_ref, *refs):
    tracked_ref = refs[0] if len(refs) == 5 else None
    clipped_out, predicted_out, inverse_out, tracked_out = refs[-4:]
    inverse = inverse_of(entries, front, front_last, back)
    inverse_out[...] = jnp.broadcast_to(inverse, (8, 128))
    for span, (one, other), rows in places(targets_ref, (front, front_last), (back, back_last)):
        tracked = (one[rows, :] + other[rows, :]) * inverse
        if tracked_ref is not None:
            tracked = momentum * tracked_ref[:, span] + tracked
        predicted = predicted_ref[:, span] - step_rate * tracked
        tracked_out[:, span] = tracked
        predicted_out[:, span] = predicted
        clipped_out[:, span] = jnp.clip(predicted - targets_ref[:, span], -huber_cap, huber_cap)


def sum_kernel(weights, *refs):
    total = jnp.zeros_like(refs[-1])
    for weight, grad_ref, inverse_ref in zip(weights, refs[:-1:2], refs[1:-1:2]):
        total = total + (weight * inverse_ref[0:1, 0:1]) * grad_ref[...]
    refs[-1][...] = total


def close_kernel(entries, weight, front, front_last, back, back_last, targets_ref, predicted_ref, tracked_ref, *refs):
    coeffs_ref, taken_ref, other_taken, grad_ref, other_grad, predicted_out, coeffs_out = refs
    inverse = inverse_of(entries, front, front_last, back)
    for span, (one, other), rows in places(targets_ref, (front, front_last), (back, back_last)):
        tracked = momentum * tracked_ref[:, span] + (one[rows, :] + other[rows, :]) * inverse
        predicted_out[:, span] = predicted_ref[:, span] - step_rate * tracked
    width = taken_ref.shape[1]
    core = lax.axis_index("paths")
    factor = weight * inverse
    for start, taken, grad in ((core, taken_ref, grad_ref), (1 - core, other_taken, other_grad)):
        span = pl.ds(pl.multiple_of(start * width, width), width)
        coeffs_out[:, span] = coeffs_ref[:, span] - (taken[...] + factor * grad[...])


def vmem(count):
    return [pl.BlockSpec(memory_space=pltpu.VMEM)] * count


def held(array):
    return pltpu.with_memory_space_constraint(array, pltpu.VMEM)


def call(kernel, name, arguments, shapes, specs=None, scratch=(), megabytes=4, aliases={}):
    shapes = tuple(shape if not isinstance(shape, tuple) else jax.ShapeDtypeStruct(shape, f32) for shape in shapes)
    return pl.pallas_call(
        kernel,
        out_shape=shapes,
        in_specs=specs or vmem(len(arguments)),
        out_specs=tuple(vmem(len(shapes))),
        scratch_shapes=scratch,
        compiler_params=pltpu.CompilerParams(vmem_limit_bytes=megabytes * 2**20),
        input_output_aliases=aliases,
        name=name,
    )(*arguments)


def shards(sizes, factors, frequency, phases, amplitude, targets, coeffs_init):
    cores, chips = sizes["paths"], sizes["feats"]
    half, risks = factors.shape
    width = frequency.shape[1] // cores
    count = targets.shape[0]
    paths = half * cores
    entries = count * width * cores * chips
    hops = [1 << bit for bit in range(chips.bit_length() - 1)]

    def swap(array):
        return lax.ppermute(array, "paths", [(0, 1), (1, 0)])

    def add(one, other):
        return call(add_kernel, "add", (one, other), (one.shape,))[0]

    def all_chips(front, back):
        orders = hops, hops[1::-1] + hops[2:]
        sums = [front, back]
        for step in range(len(hops)):
            lasts = [
                lax.ppermute(array, "feats", [(chip, chip ^ order[step]) for chip in range(chips)])
                for array, order in zip(sums, orders)
            ]
            if step < len(hops) - 1:
                sums = [add(array, last) for array, last in zip(sums, lasts)]
        return sums[0], lasts[0], sums[1], lasts[1]

    small, wide, row = (count, half), (count, width), (1, width)
    extent = count * half // 128
    middle = extent // 2
    features = pltpu.VMEM((paths, width), bf16), pltpu.VMEM((paths, width), f8)
    blanks = [
        pl.pallas_call(
            lambda out: None,
            out_shape=feature,
            out_specs=vmem(1)[0],
            compiler_params=pltpu.CompilerParams(vmem_limit_bytes=2**20),
            name=name,
        )()
        for name, feature in zip(("blank_high", "blank_low"), features)
    ]
    deep, cols = 2 * risks, divisor(width, 1024)
    own_factors, freq, start, amp = call(
        prepare_kernel,
        "prepare",
        [
            pltpu.with_memory_space_constraint(array, pltpu.HBM)
            for array in (factors, frequency, phases[None], amplitude[None], coeffs_init)
        ],
        (
            jax.ShapeDtypeStruct((half, deep), bf16),
            jax.ShapeDtypeStruct((deep, width), bf16),
            jax.ShapeDtypeStruct((2 * count, width), bf16),
            row,
        ),
        [pl.BlockSpec(memory_space=pltpu.HBM)] * 5,
        [
            pltpu.VMEM(factors.shape, factors.dtype),
            pltpu.VMEM((width // cols, risks, cols), frequency.dtype),
            pltpu.VMEM(row, phases.dtype),
            pltpu.VMEM(row, f32),
            pltpu.VMEM(wide, f32),
            pltpu.SemaphoreType.DMA((4,)),
            pltpu.SemaphoreType.DMA((width // cols,)),
        ],
        12,
    )
    image_own, image_other, high, low = call(
        build_kernel,
        "build",
        (own_factors, swap(factors), freq, start, held(blanks[0]), held(blanks[1])),
        (small, small, *features),
        None,
        [pltpu.VMEM((half, deep), bf16)],
        GRANT,
        {4: 2, 5: 3},
    )
    sums = all_chips(*call(start_kernel, "start", (image_own, swap(image_other)), ((middle, 128), (middle, 128))))
    clipped, predicted = call(open_kernel, "open", (*sums, targets), (small, small))
    weights = [step_rate * sum(momentum**later for later in range(ITERS - turn)) for turn in range(ITERS)]
    tracked = ()
    grads, inverses = [], []
    for turn in range(ITERS):
        partial = call(own_kernel, "own", (clipped, held(high), held(low)), (wide,), None, (), GRANT)[0]
        pieces = jax.ShapeDtypeStruct((2 * count, width), bf16), jax.ShapeDtypeStruct(wide, f8)
        grad, pair, coarse, image_other, notes = call(
            rest_kernel,
            "rest",
            (swap(clipped), held(high), held(low), partial, amp),
            (wide, *pieces, (extent + 8, 128), (count + 8, 128)),
            None,
            (),
            GRANT,
        )
        image_own = call(
            image_kernel, "image", (pair, coarse, notes, held(high), held(low)), ((extent + 8, 128),), None, (), GRANT
        )[0]
        halves = call(join_kernel, "join", (image_own, swap(image_other)), ((middle + 8, 128), (middle, 128)))
        grads.append(grad)
        if turn == ITERS - 1:
            break
        clipped, predicted, inverse, *tracked = call(
            functools.partial(step_kernel, entries),
            "step",
            (*all_chips(*halves), targets, predicted, *tracked),
            (small, small, (8, 128), small),
        )
        inverses.append(inverse)
    before = [array for pair in zip(grads, inverses) for array in pair]
    taken = call(functools.partial(sum_kernel, weights[:-1]), "sum", before, (wide,))[0]
    predicted, coeffs = call(
        functools.partial(close_kernel, entries, weights[-1]),
        "close",
        (*all_chips(*halves), targets, predicted, *tracked, coeffs_init, taken, swap(taken), grad, swap(grad)),
        (small, (count, width * cores)),
        None,
        (),
        8,
    )
    return (coeffs, predicted)


def solution(mesh):
    return jax.shard_map(
        functools.partial(shards, dict(mesh.shape)),
        mesh=mesh,
        in_specs=(
            P(("groups", "paths"), None),
            P(None, "feats"),
            P("feats"),
            P("feats"),
            P(None, ("groups", "paths")),
            P(None, ("groups", "feats")),
        ),
        out_specs=(P(None, ("groups", "feats")), P(None, ("groups", "paths"))),
        check_vma=False,
    )
```

profile of v0, /device:TPU:0, one launch (start us, length us, event | category | flops | bytes accessed | tf_op | source)
XLA Modules:
  0.0 132.5 jit_solution(16952931452397360787)
XLA Ops:
  1.1 2.1 %prepare.1 = (bf16[1024,256]{1,0:T(8,128)(2,1)S(1)}, bf16[256,4096]{1,0:T(8,128)(2,1)S(1)}, bf16[64,4096]{1,0:T(8,128)(2,1)S(1)}, f32[1,4096]{1,0:T(1,128)S(1)}) custom-call(s32[1024,128]{1,0:T(8,128)} %own_ref.1, s32[128,8192]{1,0:T(8,128)} %freq_ref.1, s32[1,8192]{1,0:T(1,128)} %bitcast.2, f32[1,8192]{1,0:T(1,128)} %bitcast.3, f32[32,8192]{1,0:T(8,128)} %refs_0_.1), custom_call_target="tpu_custom_call" | custom-call | tf_op jit(solution)/shard_map/prepare/pallas_call | solution.py:323
  3.3 22.1 %build.1 = (f32[32,1024]{1,0:T(8,128)S(1)}, f32[32,1024]{1,0:T(8,128)S(1)}, bf16[2048,4096]{1,0:T(8,128)(2,1)S(1)}, f8e4m3fn[2048,4096]{1,0:T(32,128)(4,1)S(1)}) custom-call(bf16[1024,256]{1,0:T(8,128)(2,1)S(1)} %get-tuple-element.45.own_ref, s32[1024,128]{1,0:T(8,128)S(1)} %collective-permute-done.other_ref, ...), custom_call_target="tpu_custom_call", output_to_operand_aliasing={{2}: (4, {}), {3}: (5, {})} | custom-call | tf_op jit(solution)/shard_map/build/pallas_call | solution.py:323
  26.9 2.7 %collective-permute-start.2 = (f32[128,128]{1,0:T(8,128)S(1)}, f32[128,128]{1,0:T(8,128)S(1)}, u32[]{:S(2)}, u32[]{:S(2)}) collective-permute-start(f32[128,128]{1,0:T(8,128)S(1)} %get-tuple-element.50.one_ref), channel_id=1, source_target_pairs={{0,1},{1,0},{2,3},{3,2},{4,5},{5,4},{6,7},{7,6},{8,9},{9,8},{10,11... | collective-permute-start | bytes 196616 | tf_op jit(solution)/shard_map/ppermute | solution.py:355
  32.2 1.9 %collective-permute-start.3 = (f32[128,128]{1,0:T(8,128)S(1)}, f32[128,128]{1,0:T(8,128)S(1)}, u32[]{:S(2)}, u32[]{:S(2)}) collective-permute-start(f32[128,128]{1,0:T(8,128)S(1)} %add.16.one_ref), channel_id=1, source_target_pairs={{0,2},{1,3},{2,0},{3,1},{4,6},{5,7},{6,4},{7,5},{8,10},{9,11},{10,... | collective-permute-start | bytes 196616 | tf_op jit(solution)/shard_map/ppermute | solution.py:355
  34.1 1.6 %collective-permute-start.6 = (f32[128,128]{1,0:T(8,128)S(1)}, f32[128,128]{1,0:T(8,128)S(1)}, u32[]{:S(2)}, u32[]{:S(2)}) collective-permute-start(f32[128,128]{1,0:T(8,128)S(1)} %add.18.one_ref), channel_id=1, source_target_pairs={{0,1},{1,0},{2,3},{3,2},{4,5},{5,4},{6,7},{7,6},{8,9},{9,8},{10,11... | collective-permute-start | bytes 196616 | tf_op jit(solution)/shard_map/ppermute | solution.py:355
  36.6 2.9 %collective-permute-start.4 = (f32[128,128]{1,0:T(8,128)S(1)}, f32[128,128]{1,0:T(8,128)S(1)}, u32[]{:S(2)}, u32[]{:S(2)}) collective-permute-start(f32[128,128]{1,0:T(8,128)S(1)} %add.17.front), channel_id=1, source_target_pairs={{0,4},{1,5},{2,6},{3,7},{4,0},{5,1},{6,2},{7,3},{8,12},{9,13},{10,... | collective-permute-start | bytes 196616 | tf_op jit(solution)/shard_map/ppermute | solution.py:355
  39.5 1.6 %collective-permute-start.7 = (f32[128,128]{1,0:T(8,128)S(1)}, f32[128,128]{1,0:T(8,128)S(1)}, u32[]{:S(2)}, u32[]{:S(2)}) collective-permute-start(f32[128,128]{1,0:T(8,128)S(1)} %add.19.back), channel_id=1, source_target_pairs={{0,4},{1,5},{2,6},{3,7},{4,0},{5,1},{6,2},{7,3},{8,12},{9,13},{10,... | collective-permute-start | bytes 196616 | tf_op jit(solution)/shard_map/ppermute | solution.py:355
  41.1 2.8 %collective-permute-done.4.front_last = f32[128,128]{1,0:T(8,128)S(1)} collective-permute-done((f32[128,128]{1,0:T(8,128)S(1)}, f32[128,128]{1,0:T(8,128)S(1)}, u32[]{:S(2)}, u32[]{:S(2)}) %collective-permute-start.4) | collective-permute-done | bytes 65568 | tf_op jit(solution)/shard_map/ppermute | solution.py:355
  44.8 2.1 %own.3.partial_ref = f32[32,4096]{1,0:T(8,128)S(1)} custom-call(f32[32,1024]{1,0:T(8,128)S(1)} %get-tuple-element.52.clipped_ref, bf16[2048,4096]{1,0:T(8,128)(2,1)S(1)} %get-tuple-element.53.high_ref, f8e4m3fn[2048,4096]{1,0:T(32,128)(4,1)S(1)} %get-tuple-element.54.low_ref), custom_call_target="tpu_custom_call" | custom-call | tf_op jit(solution)/shard_map/own/pallas_call | solution.py:323
  46.9 5.8 %rest.3 = (f32[32,4096]{1,0:T(8,128)S(1)}, bf16[64,4096]{1,0:T(8,128)(2,1)S(1)}, f8e4m3fn[32,4096]{1,0:T(32,128)(4,1)S(1)}, f32[264,128]{1,0:T(8,128)S(1)}, f32[40,128]{1,0:T(8,128)S(1)}) custom-call(f32[32,1024]{1,0:T(8,128)S(1)} %collective-permute-done.8.clipped_ref, bf16[2048,4096]{1,0:T(8,128)(2,1)S(1)} %get-tuple-element.53.high_ref, ...), custom_call_target="tpu_custom_call" | custom-call | tf_op jit(solution)/shard_map/rest/pallas_call | solution.py:323
  53.3 3.7 %image.3.own_ref = f32[264,128]{1,0:T(8,128)S(1)} custom-call(bf16[64,4096]{1,0:T(8,128)(2,1)S(1)} %get-tuple-element.56.pair_ref, f8e4m3fn[32,4096]{1,0:T(32,128)(4,1)S(1)} %get-tuple-element.57.coarse_ref, f32[40,128]{1,0:T(8,128)S(1)} %get-tuple-element.58.notes_ref, bf16[2048,4096]{1,0:T(8,128)(2,1)S(1)} %get-tuple-element.53.high_ref, ...), custom_call_target="tpu_custom_call" | custom-call | tf_op jit(solution)/shard_map/image/pallas_call | solution.py:323
  57.0 1.6 %collective-permute-start.10 = (f32[136,128]{1,0:T(8,128)S(1)}, f32[136,128]{1,0:T(8,128)S(1)}, u32[]{:S(2)}, u32[]{:S(2)}) collective-permute-start(f32[136,128]{1,0:T(8,128)S(1)} %get-tuple-element.60.one_ref), channel_id=1, source_target_pairs={{0,1},{1,0},{2,3},{3,2},{4,5},{5,4},{6,7},{7,6},{8,9},{9,8},{10,11... | collective-permute-start | bytes 208904 | tf_op jit(solution)/shard_map/ppermute | solution.py:355
  61.4 1.6 %collective-permute-start.11 = (f32[136,128]{1,0:T(8,128)S(1)}, f32[136,128]{1,0:T(8,128)S(1)}, u32[]{:S(2)}, u32[]{:S(2)}) collective-permute-start(f32[136,128]{1,0:T(8,128)S(1)} %add.20.one_ref), channel_id=1, source_target_pairs={{0,2},{1,3},{2,0},{3,1},{4,6},{5,7},{6,4},{7,5},{8,10},{9,11},{10,... | collective-permute-start | bytes 208904 | tf_op jit(solution)/shard_map/ppermute | solution.py:355
  63.1 1.6 %collective-permute-start.14 = (f32[128,128]{1,0:T(8,128)S(1)}, f32[128,128]{1,0:T(8,128)S(1)}, u32[]{:S(2)}, u32[]{:S(2)}) collective-permute-start(f32[128,128]{1,0:T(8,128)S(1)} %add.22.one_ref), channel_id=1, source_target_pairs={{0,1},{1,0},{2,3},{3,2},{4,5},{5,4},{6,7},{7,6},{8,9},{9,8},{10,11... | collective-permute-start | bytes 196616 | tf_op jit(solution)/shard_map/ppermute | solution.py:355
  65.8 1.8 %collective-permute-start.12 = (f32[136,128]{1,0:T(8,128)S(1)}, f32[136,128]{1,0:T(8,128)S(1)}, u32[]{:S(2)}, u32[]{:S(2)}) collective-permute-start(f32[136,128]{1,0:T(8,128)S(1)} %add.21.front), channel_id=1, source_target_pairs={{0,4},{1,5},{2,6},{3,7},{4,0},{5,1},{6,2},{7,3},{8,12},{9,13},{10,... | collective-permute-start | bytes 208904 | tf_op jit(solution)/shard_map/ppermute | solution.py:355
  67.6 2.0 %collective-permute-start.15 = (f32[128,128]{1,0:T(8,128)S(1)}, f32[128,128]{1,0:T(8,128)S(1)}, u32[]{:S(2)}, u32[]{:S(2)}) collective-permute-start(f32[128,128]{1,0:T(8,128)S(1)} %add.23.back), channel_id=1, source_target_pairs={{0,4},{1,5},{2,6},{3,7},{4,0},{5,1},{6,2},{7,3},{8,12},{9,13},{10,... | collective-permute-start | bytes 196616 | tf_op jit(solution)/shard_map/ppermute | solution.py:355
  69.6 3.3 %collective-permute-done.15.back_last = f32[128,128]{1,0:T(8,128)S(1)} collective-permute-done((f32[128,128]{1,0:T(8,128)S(1)}, f32[128,128]{1,0:T(8,128)S(1)}, u32[]{:S(2)}, u32[]{:S(2)}) %collective-permute-start.15) | collective-permute-done | bytes 65568 | tf_op jit(solution)/shard_map/ppermute | solution.py:355
  73.2 2.1 %own.4.partial_ref = f32[32,4096]{1,0:T(8,128)S(1)} custom-call(f32[32,1024]{1,0:T(8,128)S(1)} %get-tuple-element.63.clipped_ref, bf16[2048,4096]{1,0:T(8,128)(2,1)S(1)} %get-tuple-element.53.high_ref, f8e4m3fn[2048,4096]{1,0:T(32,128)(4,1)S(1)} %get-tuple-element.54.low_ref), custom_call_target="tpu_custom_call" | custom-call | tf_op jit(solution)/shard_map/own/pallas_call | solution.py:323
  75.3 6.0 %rest.4 = (f32[32,4096]{1,0:T(8,128)S(1)}, bf16[64,4096]{1,0:T(8,128)(2,1)S(1)}, f8e4m3fn[32,4096]{1,0:T(32,128)(4,1)S(1)}, f32[264,128]{1,0:T(8,128)S(1)}, f32[40,128]{1,0:T(8,128)S(1)}) custom-call(f32[32,1024]{1,0:T(8,128)S(1)} %collective-permute-done.16.clipped_ref, bf16[2048,4096]{1,0:T(8,128)(2,1)S(1)} %get-tuple-element.53.high_ref, ...), custom_call_target="tpu_custom_call" | custom-call | tf_op jit(solution)/shard_map/rest/pallas_call | solution.py:323
  81.9 3.7 %image.4.own_ref = f32[264,128]{1,0:T(8,128)S(1)} custom-call(bf16[64,4096]{1,0:T(8,128)(2,1)S(1)} %get-tuple-element.64.pair_ref, f8e4m3fn[32,4096]{1,0:T(32,128)(4,1)S(1)} %get-tuple-element.65.coarse_ref, f32[40,128]{1,0:T(8,128)S(1)} %get-tuple-element.66.notes_ref, bf16[2048,4096]{1,0:T(8,128)(2,1)S(1)} %get-tuple-element.53.high_ref, ...), custom_call_target="tpu_custom_call" | custom-call | tf_op jit(solution)/shard_map/image/pallas_call | solution.py:323
  85.6 1.6 %collective-permute-start.18 = (f32[136,128]{1,0:T(8,128)S(1)}, f32[136,128]{1,0:T(8,128)S(1)}, u32[]{:S(2)}, u32[]{:S(2)}) collective-permute-start(f32[136,128]{1,0:T(8,128)S(1)} %get-tuple-element.68.one_ref), channel_id=1, source_target_pairs={{0,1},{1,0},{2,3},{3,2},{4,5},{5,4},{6,7},{7,6},{8,9},{9,8},{10,11... | collective-permute-start | bytes 208904 | tf_op jit(solution)/shard_map/ppermute | solution.py:355
  87.2 1.9 %collective-permute-start.21 = (f32[128,128]{1,0:T(8,128)S(1)}, f32[128,128]{1,0:T(8,128)S(1)}, u32[]{:S(2)}, u32[]{:S(2)}) collective-permute-start(f32[128,128]{1,0:T(8,128)S(1)} %get-tuple-element.69.one_ref), channel_id=1, source_target_pairs={{0,2},{1,3},{2,0},{3,1},{4,6},{5,7},{6,4},{7,5},{8,10},{9,11},{10,... | collective-permute-start | bytes 196616 | tf_op jit(solution)/shard_map/ppermute | solution.py:355
  90.0 2.0 %collective-permute-start.19 = (f32[136,128]{1,0:T(8,128)S(1)}, f32[136,128]{1,0:T(8,128)S(1)}, u32[]{:S(2)}, u32[]{:S(2)}) collective-permute-start(f32[136,128]{1,0:T(8,128)S(1)} %add.24.one_ref), channel_id=1, source_target_pairs={{0,2},{1,3},{2,0},{3,1},{4,6},{5,7},{6,4},{7,5},{8,10},{9,11},{10,... | collective-permute-start | bytes 208904 | tf_op jit(solution)/shard_map/ppermute | solution.py:355
  94.4 2.0 %collective-permute-start.20 = (f32[136,128]{1,0:T(8,128)S(1)}, f32[136,128]{1,0:T(8,128)S(1)}, u32[]{:S(2)}, u32[]{:S(2)}) collective-permute-start(f32[136,128]{1,0:T(8,128)S(1)} %add.25.front), channel_id=1, source_target_pairs={{0,4},{1,5},{2,6},{3,7},{4,0},{5,1},{6,2},{7,3},{8,12},{9,13},{10,... | collective-permute-start | bytes 208904 | tf_op jit(solution)/shard_map/ppermute | solution.py:355
  96.4 2.0 %collective-permute-start.23 = (f32[128,128]{1,0:T(8,128)S(1)}, f32[128,128]{1,0:T(8,128)S(1)}, u32[]{:S(2)}, u32[]{:S(2)}) collective-permute-start(f32[128,128]{1,0:T(8,128)S(1)} %add.27.back), channel_id=1, source_target_pairs={{0,4},{1,5},{2,6},{3,7},{4,0},{5,1},{6,2},{7,3},{8,12},{9,13},{10,... | collective-permute-start | bytes 196616 | tf_op jit(solution)/shard_map/ppermute | solution.py:355
  98.4 3.3 %collective-permute-done.23.back_last = f32[128,128]{1,0:T(8,128)S(1)} collective-permute-done((f32[128,128]{1,0:T(8,128)S(1)}, f32[128,128]{1,0:T(8,128)S(1)}, u32[]{:S(2)}, u32[]{:S(2)}) %collective-permute-start.23) | collective-permute-done | bytes 65568 | tf_op jit(solution)/shard_map/ppermute | solution.py:355
  102.0 2.1 %own.5.partial_ref = f32[32,4096]{1,0:T(8,128)S(1)} custom-call(f32[32,1024]{1,0:T(8,128)S(1)} %get-tuple-element.72.clipped_ref, bf16[2048,4096]{1,0:T(8,128)(2,1)S(1)} %get-tuple-element.53.high_ref, f8e4m3fn[2048,4096]{1,0:T(32,128)(4,1)S(1)} %get-tuple-element.54.low_ref), custom_call_target="tpu_custom_call" | custom-call | tf_op jit(solution)/shard_map/own/pallas_call | solution.py:323
  104.8 5.8 %rest.5 = (f32[32,4096]{1,0:T(8,128)S(1)}, bf16[64,4096]{1,0:T(8,128)(2,1)S(1)}, f8e4m3fn[32,4096]{1,0:T(32,128)(4,1)S(1)}, f32[264,128]{1,0:T(8,128)S(1)}, f32[40,128]{1,0:T(8,128)S(1)}) custom-call(f32[32,1024]{1,0:T(8,128)S(1)} %collective-permute-done.24.clipped_ref, bf16[2048,4096]{1,0:T(8,128)(2,1)S(1)} %get-tuple-element.53.high_ref, ...), custom_call_target="tpu_custom_call" | custom-call | tf_op jit(solution)/shard_map/rest/pallas_call | solution.py:323
  111.2 3.7 %image.5.own_ref = f32[264,128]{1,0:T(8,128)S(1)} custom-call(bf16[64,4096]{1,0:T(8,128)(2,1)S(1)} %get-tuple-element.73.pair_ref, f8e4m3fn[32,4096]{1,0:T(32,128)(4,1)S(1)} %get-tuple-element.74.coarse_ref, f32[40,128]{1,0:T(8,128)S(1)} %get-tuple-element.75.notes_ref, bf16[2048,4096]{1,0:T(8,128)(2,1)S(1)} %get-tuple-element.53.high_ref, ...), custom_call_target="tpu_custom_call" | custom-call | tf_op jit(solution)/shard_map/image/pallas_call | solution.py:323
  119.3 2.0 %collective-permute-start.27 = (f32[136,128]{1,0:T(8,128)S(1)}, f32[136,128]{1,0:T(8,128)S(1)}, u32[]{:S(2)}, u32[]{:S(2)}) collective-permute-start(f32[136,128]{1,0:T(8,128)S(1)} %add.28.one_ref), channel_id=1, source_target_pairs={{0,2},{1,3},{2,0},{3,1},{4,6},{5,7},{6,4},{7,5},{8,10},{9,11},{10,... | collective-permute-start | bytes 208904 | tf_op jit(solution)/shard_map/ppermute | solution.py:355
  123.7 2.0 %collective-permute-start.28 = (f32[136,128]{1,0:T(8,128)S(1)}, f32[136,128]{1,0:T(8,128)S(1)}, u32[]{:S(2)}, u32[]{:S(2)}) collective-permute-start(f32[136,128]{1,0:T(8,128)S(1)} %add.29.front), channel_id=1, source_target_pairs={{0,4},{1,5},{2,6},{3,7},{4,0},{5,1},{6,2},{7,3},{8,12},{9,13},{10,... | collective-permute-start | bytes 208904 | tf_op jit(solution)/shard_map/ppermute | solution.py:355
  127.3 3.7 %collective-permute-done.31.back_last = f32[128,128]{1,0:T(8,128)S(1)} collective-permute-done((f32[128,128]{1,0:T(8,128)S(1)}, f32[128,128]{1,0:T(8,128)S(1)}, u32[]{:S(2)}, u32[]{:S(2)}) %collective-permute-start.31) | collective-permute-done | bytes 65568 | tf_op jit(solution)/shard_map/ppermute | solution.py:355
  (78 shorter events, 26.3 us)
Async XLA Ops:
  0.6 2.7 %collective-permute-start = (s32[1024,128]{1,0:T(8,128)}, s32[1024,128]{1,0:T(8,128)S(1)}, u32[]{:S(2)}, u32[]{:S(2)}) collective-permute-start(s32[1024,128]{1,0:T(8,128)} %own_ref.1), channel_id=1, source_target_pairs={{0,8},{8,0},{1,9},{9,1},{2,10},{10,2},{3,11},{11,3},{4,12},{12,4},... | collective-permute-start | bytes 1572872 | tf_op jit(solution)/shard_map/ppermute | solution.py:345
  26.9 5.3 %collective-permute-start.2 = (f32[128,128]{1,0:T(8,128)S(1)}, f32[128,128]{1,0:T(8,128)S(1)}, u32[]{:S(2)}, u32[]{:S(2)}) collective-permute-start(f32[128,128]{1,0:T(8,128)S(1)} %get-tuple-element.50.one_ref), channel_id=1, source_target_pairs={{0,1},{1,0},{2,3},{3,2},{4,5},{5,4},{6,7},{7,6},{8,9},{9,8},{10,11... | collective-permute-start | bytes 196616 | tf_op jit(solution)/shard_map/ppermute | solution.py:355
  29.6 4.5 %collective-permute-start.5 = (f32[128,128]{1,0:T(8,128)S(1)}, f32[128,128]{1,0:T(8,128)S(1)}, u32[]{:S(2)}, u32[]{:S(2)}) collective-permute-start(f32[128,128]{1,0:T(8,128)S(1)} %get-tuple-element.51.one_ref), channel_id=1, source_target_pairs={{0,2},{1,3},{2,0},{3,1},{4,6},{5,7},{6,4},{7,5},{8,10},{9,11},{10,... | collective-permute-start | bytes 196616 | tf_op jit(solution)/shard_map/ppermute | solution.py:355
  32.2 4.3 %collective-permute-start.3 = (f32[128,128]{1,0:T(8,128)S(1)}, f32[128,128]{1,0:T(8,128)S(1)}, u32[]{:S(2)}, u32[]{:S(2)}) collective-permute-start(f32[128,128]{1,0:T(8,128)S(1)} %add.16.one_ref), channel_id=1, source_target_pairs={{0,2},{1,3},{2,0},{3,1},{4,6},{5,7},{6,4},{7,5},{8,10},{9,11},{10,... | collective-permute-start | bytes 196616 | tf_op jit(solution)/shard_map/ppermute | solution.py:355
  34.1 5.3 %collective-permute-start.6 = (f32[128,128]{1,0:T(8,128)S(1)}, f32[128,128]{1,0:T(8,128)S(1)}, u32[]{:S(2)}, u32[]{:S(2)}) collective-permute-start(f32[128,128]{1,0:T(8,128)S(1)} %add.18.one_ref), channel_id=1, source_target_pairs={{0,1},{1,0},{2,3},{3,2},{4,5},{5,4},{6,7},{7,6},{8,9},{9,8},{10,11... | collective-permute-start | bytes 196616 | tf_op jit(solution)/shard_map/ppermute | solution.py:355
  36.6 7.3 %collective-permute-start.4 = (f32[128,128]{1,0:T(8,128)S(1)}, f32[128,128]{1,0:T(8,128)S(1)}, u32[]{:S(2)}, u32[]{:S(2)}) collective-permute-start(f32[128,128]{1,0:T(8,128)S(1)} %add.17.front), channel_id=1, source_target_pairs={{0,4},{1,5},{2,6},{3,7},{4,0},{5,1},{6,2},{7,3},{8,12},{9,13},{10,... | collective-permute-start | bytes 196616 | tf_op jit(solution)/shard_map/ppermute | solution.py:355
  39.5 5.2 %collective-permute-start.7 = (f32[128,128]{1,0:T(8,128)S(1)}, f32[128,128]{1,0:T(8,128)S(1)}, u32[]{:S(2)}, u32[]{:S(2)}) collective-permute-start(f32[128,128]{1,0:T(8,128)S(1)} %add.19.back), channel_id=1, source_target_pairs={{0,4},{1,5},{2,6},{3,7},{4,0},{5,1},{6,2},{7,3},{8,12},{9,13},{10,... | collective-permute-start | bytes 196616 | tf_op jit(solution)/shard_map/ppermute | solution.py:355
  44.7 2.2 %collective-permute-start.8 = (f32[32,1024]{1,0:T(8,128)S(1)}, f32[32,1024]{1,0:T(8,128)S(1)}, u32[]{:S(2)}, u32[]{:S(2)}) collective-permute-start(f32[32,1024]{1,0:T(8,128)S(1)} %get-tuple-element.52.clipped_ref), channel_id=1, source_target_pairs={{0,8},{8,0},{1,9},{9,1},{2,10},{10,2},{3,11},{11,3},{4,12},{12,4},... | collective-permute-start | bytes 393224 | tf_op jit(solution)/shard_map/ppermute | solution.py:345
  52.8 4.2 %collective-permute-start.9 = (f32[264,128]{1,0:T(8,128)S(1)}, f32[264,128]{1,0:T(8,128)S(1)}, u32[]{:S(2)}, u32[]{:S(2)}) collective-permute-start(f32[264,128]{1,0:T(8,128)S(1)} %get-tuple-element.59), channel_id=1, source_target_pairs={{0,8},{8,0},{1,9},{9,1},{2,10},{10,2},{3,11},{11,3},{4,12},{12,4},... | collective-permute-start | bytes 405512 | tf_op jit(solution)/shard_map/ppermute | solution.py:345
  57.0 4.4 %collective-permute-start.10 = (f32[136,128]{1,0:T(8,128)S(1)}, f32[136,128]{1,0:T(8,128)S(1)}, u32[]{:S(2)}, u32[]{:S(2)}) collective-permute-start(f32[136,128]{1,0:T(8,128)S(1)} %get-tuple-element.60.one_ref), channel_id=1, source_target_pairs={{0,1},{1,0},{2,3},{3,2},{4,5},{5,4},{6,7},{7,6},{8,9},{9,8},{10,11... | collective-permute-start | bytes 208904 | tf_op jit(solution)/shard_map/ppermute | solution.py:355
  58.6 4.4 %collective-permute-start.13 = (f32[128,128]{1,0:T(8,128)S(1)}, f32[128,128]{1,0:T(8,128)S(1)}, u32[]{:S(2)}, u32[]{:S(2)}) collective-permute-start(f32[128,128]{1,0:T(8,128)S(1)} %get-tuple-element.61.one_ref), channel_id=1, source_target_pairs={{0,2},{1,3},{2,0},{3,1},{4,6},{5,7},{6,4},{7,5},{8,10},{9,11},{10,... | collective-permute-start | bytes 196616 | tf_op jit(solution)/shard_map/ppermute | solution.py:355
  61.4 4.4 %collective-permute-start.11 = (f32[136,128]{1,0:T(8,128)S(1)}, f32[136,128]{1,0:T(8,128)S(1)}, u32[]{:S(2)}, u32[]{:S(2)}) collective-permute-start(f32[136,128]{1,0:T(8,128)S(1)} %add.20.one_ref), channel_id=1, source_target_pairs={{0,2},{1,3},{2,0},{3,1},{4,6},{5,7},{6,4},{7,5},{8,10},{9,11},{10,... | collective-permute-start | bytes 208904 | tf_op jit(solution)/shard_map/ppermute | solution.py:355
  63.1 4.5 %collective-permute-start.14 = (f32[128,128]{1,0:T(8,128)S(1)}, f32[128,128]{1,0:T(8,128)S(1)}, u32[]{:S(2)}, u32[]{:S(2)}) collective-permute-start(f32[128,128]{1,0:T(8,128)S(1)} %add.22.one_ref), channel_id=1, source_target_pairs={{0,1},{1,0},{2,3},{3,2},{4,5},{5,4},{6,7},{7,6},{8,9},{9,8},{10,11... | collective-permute-start | bytes 196616 | tf_op jit(solution)/shard_map/ppermute | solution.py:355
  65.8 7.1 %collective-permute-start.12 = (f32[136,128]{1,0:T(8,128)S(1)}, f32[136,128]{1,0:T(8,128)S(1)}, u32[]{:S(2)}, u32[]{:S(2)}) collective-permute-start(f32[136,128]{1,0:T(8,128)S(1)} %add.21.front), channel_id=1, source_target_pairs={{0,4},{1,5},{2,6},{3,7},{4,0},{5,1},{6,2},{7,3},{8,12},{9,13},{10,... | collective-permute-start | bytes 208904 | tf_op jit(solution)/shard_map/ppermute | solution.py:355
  67.6 5.3 %collective-permute-start.15 = (f32[128,128]{1,0:T(8,128)S(1)}, f32[128,128]{1,0:T(8,128)S(1)}, u32[]{:S(2)}, u32[]{:S(2)}) collective-permute-start(f32[128,128]{1,0:T(8,128)S(1)} %add.23.back), channel_id=1, source_target_pairs={{0,4},{1,5},{2,6},{3,7},{4,0},{5,1},{6,2},{7,3},{8,12},{9,13},{10,... | collective-permute-start | bytes 196616 | tf_op jit(solution)/shard_map/ppermute | solution.py:355
  81.3 4.2 %collective-permute-start.17 = (f32[264,128]{1,0:T(8,128)S(1)}, f32[264,128]{1,0:T(8,128)S(1)}, u32[]{:S(2)}, u32[]{:S(2)}) collective-permute-start(f32[264,128]{1,0:T(8,128)S(1)} %get-tuple-element.67), channel_id=1, source_target_pairs={{0,8},{8,0},{1,9},{9,1},{2,10},{10,2},{3,11},{11,3},{4,12},{12,4},... | collective-permute-start | bytes 405512 | tf_op jit(solution)/shard_map/ppermute | solution.py:345
  85.6 4.4 %collective-permute-start.18 = (f32[136,128]{1,0:T(8,128)S(1)}, f32[136,128]{1,0:T(8,128)S(1)}, u32[]{:S(2)}, u32[]{:S(2)}) collective-permute-start(f32[136,128]{1,0:T(8,128)S(1)} %get-tuple-element.68.one_ref), channel_id=1, source_target_pairs={{0,1},{1,0},{2,3},{3,2},{4,5},{5,4},{6,7},{7,6},{8,9},{9,8},{10,11... | collective-permute-start | bytes 208904 | tf_op jit(solution)/shard_map/ppermute | solution.py:355
  87.2 4.8 %collective-permute-start.21 = (f32[128,128]{1,0:T(8,128)S(1)}, f32[128,128]{1,0:T(8,128)S(1)}, u32[]{:S(2)}, u32[]{:S(2)}) collective-permute-start(f32[128,128]{1,0:T(8,128)S(1)} %get-tuple-element.69.one_ref), channel_id=1, source_target_pairs={{0,2},{1,3},{2,0},{3,1},{4,6},{5,7},{6,4},{7,5},{8,10},{9,11},{10,... | collective-permute-start | bytes 196616 | tf_op jit(solution)/shard_map/ppermute | solution.py:355
  90.0 4.4 %collective-permute-start.19 = (f32[136,128]{1,0:T(8,128)S(1)}, f32[136,128]{1,0:T(8,128)S(1)}, u32[]{:S(2)}, u32[]{:S(2)}) collective-permute-start(f32[136,128]{1,0:T(8,128)S(1)} %add.24.one_ref), channel_id=1, source_target_pairs={{0,2},{1,3},{2,0},{3,1},{4,6},{5,7},{6,4},{7,5},{8,10},{9,11},{10,... | collective-permute-start | bytes 208904 | tf_op jit(solution)/shard_map/ppermute | solution.py:355
  92.0 4.4 %collective-permute-start.22 = (f32[128,128]{1,0:T(8,128)S(1)}, f32[128,128]{1,0:T(8,128)S(1)}, u32[]{:S(2)}, u32[]{:S(2)}) collective-permute-start(f32[128,128]{1,0:T(8,128)S(1)} %add.26.one_ref), channel_id=1, source_target_pairs={{0,1},{1,0},{2,3},{3,2},{4,5},{5,4},{6,7},{7,6},{8,9},{9,8},{10,11... | collective-permute-start | bytes 196616 | tf_op jit(solution)/shard_map/ppermute | solution.py:355
  94.4 7.4 %collective-permute-start.20 = (f32[136,128]{1,0:T(8,128)S(1)}, f32[136,128]{1,0:T(8,128)S(1)}, u32[]{:S(2)}, u32[]{:S(2)}) collective-permute-start(f32[136,128]{1,0:T(8,128)S(1)} %add.25.front), channel_id=1, source_target_pairs={{0,4},{1,5},{2,6},{3,7},{4,0},{5,1},{6,2},{7,3},{8,12},{9,13},{10,... | collective-permute-start | bytes 208904 | tf_op jit(solution)/shard_map/ppermute | solution.py:355
  96.4 5.3 %collective-permute-start.23 = (f32[128,128]{1,0:T(8,128)S(1)}, f32[128,128]{1,0:T(8,128)S(1)}, u32[]{:S(2)}, u32[]{:S(2)}) collective-permute-start(f32[128,128]{1,0:T(8,128)S(1)} %add.27.back), channel_id=1, source_target_pairs={{0,4},{1,5},{2,6},{3,7},{4,0},{5,1},{6,2},{7,3},{8,12},{9,13},{10,... | collective-permute-start | bytes 196616 | tf_op jit(solution)/shard_map/ppermute | solution.py:355
  101.9 2.9 %collective-permute-start.24 = (f32[32,1024]{1,0:T(8,128)S(1)}, f32[32,1024]{1,0:T(8,128)S(1)}, u32[]{:S(2)}, u32[]{:S(2)}) collective-permute-start(f32[32,1024]{1,0:T(8,128)S(1)} %get-tuple-element.72.clipped_ref), channel_id=1, source_target_pairs={{0,8},{8,0},{1,9},{9,1},{2,10},{10,2},{3,11},{11,3},{4,12},{12,4},... | collective-permute-start | bytes 393224 | tf_op jit(solution)/shard_map/ppermute | solution.py:345
  104.3 26.8 %collective-permute-start.32 = (f32[32,4096]{1,0:T(8,128)S(1)}, f32[32,4096]{1,0:T(8,128)S(1)}, u32[]{:S(2)}, u32[]{:S(2)}) collective-permute-start(f32[32,4096]{1,0:T(8,128)S(1)} %sum.1.refs_1_), channel_id=1, source_target_pairs={{0,8},{8,0},{1,9},{9,1},{2,10},{10,2},{3,11},{11,3},{4,12},{12,4},... | collective-permute-start | bytes 1572872 | tf_op jit(solution)/shard_map/ppermute | solution.py:345
  110.7 20.4 %collective-permute-start.33 = (f32[32,4096]{1,0:T(8,128)S(1)}, f32[32,4096]{1,0:T(8,128)S(1)}, u32[]{:S(2)}, u32[]{:S(2)}) collective-permute-start(f32[32,4096]{1,0:T(8,128)S(1)} %get-tuple-element.85.refs_3_), channel_id=1, source_target_pairs={{0,8},{8,0},{1,9},{9,1},{2,10},{10,2},{3,11},{11,3},{4,12},{12,4},... | collective-permute-start | bytes 1572872 | tf_op jit(solution)/shard_map/ppermute | solution.py:345
  110.7 4.2 %collective-permute-start.25 = (f32[264,128]{1,0:T(8,128)S(1)}, f32[264,128]{1,0:T(8,128)S(1)}, u32[]{:S(2)}, u32[]{:S(2)}) collective-permute-start(f32[264,128]{1,0:T(8,128)S(1)} %get-tuple-element.76), channel_id=1, source_target_pairs={{0,8},{8,0},{1,9},{9,1},{2,10},{10,2},{3,11},{11,3},{4,12},{12,4},... | collective-permute-start | bytes 405512 | tf_op jit(solution)/shard_map/ppermute | solution.py:345
  114.9 4.4 %collective-permute-start.26 = (f32[136,128]{1,0:T(8,128)S(1)}, f32[136,128]{1,0:T(8,128)S(1)}, u32[]{:S(2)}, u32[]{:S(2)}) collective-permute-start(f32[136,128]{1,0:T(8,128)S(1)} %get-tuple-element.77.one_ref), channel_id=1, source_target_pairs={{0,1},{1,0},{2,3},{3,2},{4,5},{5,4},{6,7},{7,6},{8,9},{9,8},{10,11... | collective-permute-start | bytes 208904 | tf_op jit(solution)/shard_map/ppermute | solution.py:355
  116.5 4.8 %collective-permute-start.29 = (f32[128,128]{1,0:T(8,128)S(1)}, f32[128,128]{1,0:T(8,128)S(1)}, u32[]{:S(2)}, u32[]{:S(2)}) collective-permute-start(f32[128,128]{1,0:T(8,128)S(1)} %get-tuple-element.78.one_ref), channel_id=1, source_target_pairs={{0,2},{1,3},{2,0},{3,1},{4,6},{5,7},{6,4},{7,5},{8,10},{9,11},{10,... | collective-permute-start | bytes 196616 | tf_op jit(solution)/shard_map/ppermute | solution.py:355
  119.3 4.4 %collective-permute-start.27 = (f32[136,128]{1,0:T(8,128)S(1)}, f32[136,128]{1,0:T(8,128)S(1)}, u32[]{:S(2)}, u32[]{:S(2)}) collective-permute-start(f32[136,128]{1,0:T(8,128)S(1)} %add.28.one_ref), channel_id=1, source_target_pairs={{0,2},{1,3},{2,0},{3,1},{4,6},{5,7},{6,4},{7,5},{8,10},{9,11},{10,... | collective-permute-start | bytes 208904 | tf_op jit(solution)/shard_map/ppermute | solution.py:355
  121.3 4.4 %collective-permute-start.30 = (f32[128,128]{1,0:T(8,128)S(1)}, f32[128,128]{1,0:T(8,128)S(1)}, u32[]{:S(2)}, u32[]{:S(2)}) collective-permute-start(f32[128,128]{1,0:T(8,128)S(1)} %add.30.one_ref), channel_id=1, source_target_pairs={{0,1},{1,0},{2,3},{3,2},{4,5},{5,4},{6,7},{7,6},{8,9},{9,8},{10,11... | collective-permute-start | bytes 196616 | tf_op jit(solution)/shard_map/ppermute | solution.py:355
  123.7 7.3 %collective-permute-start.28 = (f32[136,128]{1,0:T(8,128)S(1)}, f32[136,128]{1,0:T(8,128)S(1)}, u32[]{:S(2)}, u32[]{:S(2)}) collective-permute-start(f32[136,128]{1,0:T(8,128)S(1)} %add.29.front), channel_id=1, source_target_pairs={{0,4},{1,5},{2,6},{3,7},{4,0},{5,1},{6,2},{7,3},{8,12},{9,13},{10,... | collective-permute-start | bytes 208904 | tf_op jit(solution)/shard_map/ppermute | solution.py:355
  125.8 5.3 %collective-permute-start.31 = (f32[128,128]{1,0:T(8,128)S(1)}, f32[128,128]{1,0:T(8,128)S(1)}, u32[]{:S(2)}, u32[]{:S(2)}) collective-permute-start(f32[128,128]{1,0:T(8,128)S(1)} %add.31.back), channel_id=1, source_target_pairs={{0,4},{1,5},{2,6},{3,7},{4,0},{5,1},{6,2},{7,3},{8,12},{9,13},{10,... | collective-permute-start | bytes 196616 | tf_op jit(solution)/shard_map/ppermute | solution.py:355
  (4 other events, 64.9 us)
where the time goes:
time: 133 us; the launch traced here: 132 us
  Pallas kernels  61.5 us (46%)
  starting transfers between devices  46.1 us (35%)
  waiting for transfers between devices  23.9 us (18%)
    pallas_call x36, Pallas kernels, call(): pl.pallas_call(kernel, out_shape=shapes, in_specs=specs or vmem(len(argum...  61.5 us
    ppermute x24, starting transfers between devices, all_chips(): lax.ppermute(array, 'feats', [(chip, chip ^ order[step]) for chip in rang...  43.2 us
    ppermute x24, waiting for transfers between devices, all_chips(): lax.ppermute(array, 'feats', [(chip, chip ^ order[step]) for chip in rang...  22.6 us
    ppermute x10, starting transfers between devices, swap(): return lax.ppermute(array, 'paths', [(0, 1), (1, 0)])  2.98 us
  transfers between devices with their start and end apart: 34, of which 14 were waited for; matrix products, arithmetic and copies ran while one was open for 0% of the time, Pallas kernels for 19%

commit v1 on v0

--- a/solution.py
+++ b/solution.py
@@ -176,13 +176,16 @@
     return main[:count] + main[count:] + rest * (1.0 / (CLIP * LOW))
 
 
-def image_of(pair_ref, coarse_ref, level, high_ref, low_ref, place, image_ref):
-    count = pair_ref.shape[0] // 2
-    main = lax.dot_general(pair_ref[...], high_ref[place, :], NT, preferred_element_type=f32)
-    rest = lax.dot_general(coarse_ref[...], low_ref[place, :], NT, preferred_element_type=f32)
-    image = main[:count] + main[count:] + rest * (level * (1.0 / LOW))
-    for tile in range(image.shape[1] // 128):
-        image_ref[pl.ds(tile * count, count), :] = image[:, tile * 128 : tile * 128 + 128]
+def image_of(pair_ref, coarse_ref, level, high_ref, low_ref, start, image_ref):
+    count, half = pair_ref.shape[0] // 2, high_ref.shape[0] // 2
+    rows = divisor(half, 512)
+    for first in range(0, half, rows):
+        place = pl.ds(start + first, rows)
+        main = lax.dot_general(high_ref[place, :], pair_ref[...], NT, preferred_element_type=f32).T
+        rest = lax.dot_general(coarse_ref[...], low_ref[place, :], NT, preferred_element_type=f32)
+        image = main[:count] + main[count:] + rest * (level * (1.0 / LOW))
+        for lane in range(0, rows, 128):
+            image_ref[pl.ds((first + lane) // 128 * count, count), :] = image[:, lane : lane + 128]
 
 
 def own_kernel(clipped_ref, high_ref, low_ref, partial_out):
@@ -221,7 +224,7 @@
     for index in range(width // cols):
         span = pl.ds(index * cols, cols)
         coarse_out[:, span] = (pair_out[:count, span].astype(f32) * (1.0 / level)).astype(f8)
-    image_of(pair_out, coarse_out, level, high_ref, low_ref, pl.ds(half, half), image_out)
+    image_of(pair_out, coarse_out, level, high_ref, low_ref, half, image_out)
     image_out[pl.ds(count * half // 128, 8), :] = squares
     notes_out[:8, :] = squares
     notes_out[8:, :] = jnp.broadcast_to(level, (count, 128))
@@ -229,7 +232,7 @@
 
 def image_kernel(pair_ref, coarse_ref, notes_ref, high_ref, low_ref, image_out):
     half = high_ref.shape[0] // 2
-    image_of(pair_ref, coarse_ref, notes_ref[8:, :1], high_ref, low_ref, pl.ds(0, half), image_out)
+    image_of(pair_ref, coarse_ref, notes_ref[8:, :1], high_ref, low_ref, 0, image_out)
     image_out[pl.ds(pair_ref.shape[0] // 2 * half // 128, 8), :] = notes_ref[:8, :]
 
 

time: 133 us -> 132 us (level)
  no operation moved by 1% of the time
where the time goes in v1:
time: 132 us; the launch traced here: 131 us
  Pallas kernels  60.3 us (46%)
  starting transfers between devices  46.3 us (35%)
  waiting for transfers between devices  23.9 us (18%)
    pallas_call x36, Pallas kernels, call(): pl.pallas_call(kernel, out_shape=shapes, in_specs=specs or vmem(len(argum...  60.3 us
    ppermute x24, starting transfers between devices, all_chips(): lax.ppermute(array, 'feats', [(chip, chip ^ order[step]) for chip in rang...  43.2 us
    ppermute x24, waiting for transfers between devices, all_chips(): lax.ppermute(array, 'feats', [(chip, chip ^ order[step]) for chip in rang...  22.6 us
    ppermute x10, starting transfers between devices, swap(): return lax.ppermute(array, 'paths', [(0, 1), (1, 0)])  3.13 us
  transfers between devices with their start and end apart: 34, of which 14 were waited for; matrix products, arithmetic and copies ran while one was open for 0% of the time, Pallas kernels for 19%

profile of v1, /device:TPU:0, one launch (start us, length us, event | category | flops | bytes accessed | tf_op | source)
XLA Modules:
  0.0 131.4 jit_solution(10778946374942091421)
XLA Ops:
  1.1 2.1 %prepare.1 = (bf16[1024,256]{1,0:T(8,128)(2,1)S(1)}, bf16[256,4096]{1,0:T(8,128)(2,1)S(1)}, bf16[64,4096]{1,0:T(8,128)(2,1)S(1)}, f32[1,4096]{1,0:T(1,128)S(1)}) custom-call(s32[1024,128]{1,0:T(8,128)} %own_ref.1, s32[128,8192]{1,0:T(8,128)} %freq_ref.1, s32[1,8192]{1,0:T(1,128)} %bitcast.2, f32[1,8192]{1,0:T(1,128)} %bitcast.3, f32[32,8192]{1,0:T(8,128)} %refs_0_.1), custom_call_target="tpu_custom_call" | custom-call | tf_op jit(solution)/shard_map/prepare/pallas_call | solution.py:326
  3.3 22.1 %build.1 = (f32[32,1024]{1,0:T(8,128)S(1)}, f32[32,1024]{1,0:T(8,128)S(1)}, bf16[2048,4096]{1,0:T(8,128)(2,1)S(1)}, f8e4m3fn[2048,4096]{1,0:T(32,128)(4,1)S(1)}) custom-call(bf16[1024,256]{1,0:T(8,128)(2,1)S(1)} %get-tuple-element.45.own_ref, s32[1024,128]{1,0:T(8,128)S(1)} %collective-permute-done.other_ref, ...), custom_call_target="tpu_custom_call", output_to_operand_aliasing={{2}: (4, {}), {3}: (5, {})} | custom-call | tf_op jit(solution)/shard_map/build/pallas_call | solution.py:326
  26.9 2.7 %collective-permute-start.2 = (f32[128,128]{1,0:T(8,128)S(1)}, f32[128,128]{1,0:T(8,128)S(1)}, u32[]{:S(2)}, u32[]{:S(2)}) collective-permute-start(f32[128,128]{1,0:T(8,128)S(1)} %get-tuple-element.50.one_ref), channel_id=1, source_target_pairs={{0,1},{1,0},{2,3},{3,2},{4,5},{5,4},{6,7},{7,6},{8,9},{9,8},{10,11... | collective-permute-start | bytes 196616 | tf_op jit(solution)/shard_map/ppermute | solution.py:358
  32.2 1.9 %collective-permute-start.3 = (f32[128,128]{1,0:T(8,128)S(1)}, f32[128,128]{1,0:T(8,128)S(1)}, u32[]{:S(2)}, u32[]{:S(2)}) collective-permute-start(f32[128,128]{1,0:T(8,128)S(1)} %add.16.one_ref), channel_id=1, source_target_pairs={{0,2},{1,3},{2,0},{3,1},{4,6},{5,7},{6,4},{7,5},{8,10},{9,11},{10,... | collective-permute-start | bytes 196616 | tf_op jit(solution)/shard_map/ppermute | solution.py:358
  34.1 1.6 %collective-permute-start.6 = (f32[128,128]{1,0:T(8,128)S(1)}, f32[128,128]{1,0:T(8,128)S(1)}, u32[]{:S(2)}, u32[]{:S(2)}) collective-permute-start(f32[128,128]{1,0:T(8,128)S(1)} %add.18.one_ref), channel_id=1, source_target_pairs={{0,1},{1,0},{2,3},{3,2},{4,5},{5,4},{6,7},{7,6},{8,9},{9,8},{10,11... | collective-permute-start | bytes 196616 | tf_op jit(solution)/shard_map/ppermute | solution.py:358
  36.6 2.9 %collective-permute-start.4 = (f32[128,128]{1,0:T(8,128)S(1)}, f32[128,128]{1,0:T(8,128)S(1)}, u32[]{:S(2)}, u32[]{:S(2)}) collective-permute-start(f32[128,128]{1,0:T(8,128)S(1)} %add.17.front), channel_id=1, source_target_pairs={{0,4},{1,5},{2,6},{3,7},{4,0},{5,1},{6,2},{7,3},{8,12},{9,13},{10,... | collective-permute-start | bytes 196616 | tf_op jit(solution)/shard_map/ppermute | solution.py:358
  39.5 1.6 %collective-permute-start.7 = (f32[128,128]{1,0:T(8,128)S(1)}, f32[128,128]{1,0:T(8,128)S(1)}, u32[]{:S(2)}, u32[]{:S(2)}) collective-permute-start(f32[128,128]{1,0:T(8,128)S(1)} %add.19.back), channel_id=1, source_target_pairs={{0,4},{1,5},{2,6},{3,7},{4,0},{5,1},{6,2},{7,3},{8,12},{9,13},{10,... | collective-permute-start | bytes 196616 | tf_op jit(solution)/shard_map/ppermute | solution.py:358
  41.1 2.8 %collective-permute-done.4.front_last = f32[128,128]{1,0:T(8,128)S(1)} collective-permute-done((f32[128,128]{1,0:T(8,128)S(1)}, f32[128,128]{1,0:T(8,128)S(1)}, u32[]{:S(2)}, u32[]{:S(2)}) %collective-permute-start.4) | collective-permute-done | bytes 65568 | tf_op jit(solution)/shard_map/ppermute | solution.py:358
  44.8 2.1 %own.3.partial_ref = f32[32,4096]{1,0:T(8,128)S(1)} custom-call(f32[32,1024]{1,0:T(8,128)S(1)} %get-tuple-element.52.clipped_ref, bf16[2048,4096]{1,0:T(8,128)(2,1)S(1)} %get-tuple-element.53.high_ref, f8e4m3fn[2048,4096]{1,0:T(32,128)(4,1)S(1)} %get-tuple-element.54.low_ref), custom_call_target="tpu_custom_call" | custom-call | tf_op jit(solution)/shard_map/own/pallas_call | solution.py:326
  46.9 5.7 %rest.3 = (f32[32,4096]{1,0:T(8,128)S(1)}, bf16[64,4096]{1,0:T(8,128)(2,1)S(1)}, f8e4m3fn[32,4096]{1,0:T(32,128)(4,1)S(1)}, f32[264,128]{1,0:T(8,128)S(1)}, f32[40,128]{1,0:T(8,128)S(1)}) custom-call(f32[32,1024]{1,0:T(8,128)S(1)} %collective-permute-done.8.clipped_ref, bf16[2048,4096]{1,0:T(8,128)(2,1)S(1)} %get-tuple-element.53.high_ref, ...), custom_call_target="tpu_custom_call" | custom-call | tf_op jit(solution)/shard_map/rest/pallas_call | solution.py:326
  53.2 3.4 %image.3.own_ref = f32[264,128]{1,0:T(8,128)S(1)} custom-call(bf16[64,4096]{1,0:T(8,128)(2,1)S(1)} %get-tuple-element.56.pair_ref, f8e4m3fn[32,4096]{1,0:T(32,128)(4,1)S(1)} %get-tuple-element.57.coarse_ref, f32[40,128]{1,0:T(8,128)S(1)} %get-tuple-element.58.notes_ref, bf16[2048,4096]{1,0:T(8,128)(2,1)S(1)} %get-tuple-element.53.high_ref, ...), custom_call_target="tpu_custom_call" | custom-call | tf_op jit(solution)/shard_map/image/pallas_call | solution.py:326
  56.7 1.6 %collective-permute-start.10 = (f32[136,128]{1,0:T(8,128)S(1)}, f32[136,128]{1,0:T(8,128)S(1)}, u32[]{:S(2)}, u32[]{:S(2)}) collective-permute-start(f32[136,128]{1,0:T(8,128)S(1)} %get-tuple-element.60.one_ref), channel_id=1, source_target_pairs={{0,1},{1,0},{2,3},{3,2},{4,5},{5,4},{6,7},{7,6},{8,9},{9,8},{10,11... | collective-permute-start | bytes 208904 | tf_op jit(solution)/shard_map/ppermute | solution.py:358
  61.1 1.6 %collective-permute-start.11 = (f32[136,128]{1,0:T(8,128)S(1)}, f32[136,128]{1,0:T(8,128)S(1)}, u32[]{:S(2)}, u32[]{:S(2)}) collective-permute-start(f32[136,128]{1,0:T(8,128)S(1)} %add.20.one_ref), channel_id=1, source_target_pairs={{0,2},{1,3},{2,0},{3,1},{4,6},{5,7},{6,4},{7,5},{8,10},{9,11},{10,... | collective-permute-start | bytes 208904 | tf_op jit(solution)/shard_map/ppermute | solution.py:358
  62.7 1.6 %collective-permute-start.14 = (f32[128,128]{1,0:T(8,128)S(1)}, f32[128,128]{1,0:T(8,128)S(1)}, u32[]{:S(2)}, u32[]{:S(2)}) collective-permute-start(f32[128,128]{1,0:T(8,128)S(1)} %add.22.one_ref), channel_id=1, source_target_pairs={{0,1},{1,0},{2,3},{3,2},{4,5},{5,4},{6,7},{7,6},{8,9},{9,8},{10,11... | collective-permute-start | bytes 196616 | tf_op jit(solution)/shard_map/ppermute | solution.py:358
  65.5 1.8 %collective-permute-start.12 = (f32[136,128]{1,0:T(8,128)S(1)}, f32[136,128]{1,0:T(8,128)S(1)}, u32[]{:S(2)}, u32[]{:S(2)}) collective-permute-start(f32[136,128]{1,0:T(8,128)S(1)} %add.21.front), channel_id=1, source_target_pairs={{0,4},{1,5},{2,6},{3,7},{4,0},{5,1},{6,2},{7,3},{8,12},{9,13},{10,... | collective-permute-start | bytes 208904 | tf_op jit(solution)/shard_map/ppermute | solution.py:358
  67.2 2.0 %collective-permute-start.15 = (f32[128,128]{1,0:T(8,128)S(1)}, f32[128,128]{1,0:T(8,128)S(1)}, u32[]{:S(2)}, u32[]{:S(2)}) collective-permute-start(f32[128,128]{1,0:T(8,128)S(1)} %add.23.back), channel_id=1, source_target_pairs={{0,4},{1,5},{2,6},{3,7},{4,0},{5,1},{6,2},{7,3},{8,12},{9,13},{10,... | collective-permute-start | bytes 196616 | tf_op jit(solution)/shard_map/ppermute | solution.py:358
  69.3 3.3 %collective-permute-done.15.back_last = f32[128,128]{1,0:T(8,128)S(1)} collective-permute-done((f32[128,128]{1,0:T(8,128)S(1)}, f32[128,128]{1,0:T(8,128)S(1)}, u32[]{:S(2)}, u32[]{:S(2)}) %collective-permute-start.15) | collective-permute-done | bytes 65568 | tf_op jit(solution)/shard_map/ppermute | solution.py:358
  72.8 2.1 %own.4.partial_ref = f32[32,4096]{1,0:T(8,128)S(1)} custom-call(f32[32,1024]{1,0:T(8,128)S(1)} %get-tuple-element.63.clipped_ref, bf16[2048,4096]{1,0:T(8,128)(2,1)S(1)} %get-tuple-element.53.high_ref, f8e4m3fn[2048,4096]{1,0:T(32,128)(4,1)S(1)} %get-tuple-element.54.low_ref), custom_call_target="tpu_custom_call" | custom-call | tf_op jit(solution)/shard_map/own/pallas_call | solution.py:326
  75.0 5.9 %rest.4 = (f32[32,4096]{1,0:T(8,128)S(1)}, bf16[64,4096]{1,0:T(8,128)(2,1)S(1)}, f8e4m3fn[32,4096]{1,0:T(32,128)(4,1)S(1)}, f32[264,128]{1,0:T(8,128)S(1)}, f32[40,128]{1,0:T(8,128)S(1)}) custom-call(f32[32,1024]{1,0:T(8,128)S(1)} %collective-permute-done.16.clipped_ref, bf16[2048,4096]{1,0:T(8,128)(2,1)S(1)} %get-tuple-element.53.high_ref, ...), custom_call_target="tpu_custom_call" | custom-call | tf_op jit(solution)/shard_map/rest/pallas_call | solution.py:326
  81.4 3.4 %image.4.own_ref = f32[264,128]{1,0:T(8,128)S(1)} custom-call(bf16[64,4096]{1,0:T(8,128)(2,1)S(1)} %get-tuple-element.64.pair_ref, f8e4m3fn[32,4096]{1,0:T(32,128)(4,1)S(1)} %get-tuple-element.65.coarse_ref, f32[40,128]{1,0:T(8,128)S(1)} %get-tuple-element.66.notes_ref, bf16[2048,4096]{1,0:T(8,128)(2,1)S(1)} %get-tuple-element.53.high_ref, ...), custom_call_target="tpu_custom_call" | custom-call | tf_op jit(solution)/shard_map/image/pallas_call | solution.py:326
  84.9 1.6 %collective-permute-start.18 = (f32[136,128]{1,0:T(8,128)S(1)}, f32[136,128]{1,0:T(8,128)S(1)}, u32[]{:S(2)}, u32[]{:S(2)}) collective-permute-start(f32[136,128]{1,0:T(8,128)S(1)} %get-tuple-element.68.one_ref), channel_id=1, source_target_pairs={{0,1},{1,0},{2,3},{3,2},{4,5},{5,4},{6,7},{7,6},{8,9},{9,8},{10,11... | collective-permute-start | bytes 208904 | tf_op jit(solution)/shard_map/ppermute | solution.py:358
  86.5 1.9 %collective-permute-start.21 = (f32[128,128]{1,0:T(8,128)S(1)}, f32[128,128]{1,0:T(8,128)S(1)}, u32[]{:S(2)}, u32[]{:S(2)}) collective-permute-start(f32[128,128]{1,0:T(8,128)S(1)} %get-tuple-element.69.one_ref), channel_id=1, source_target_pairs={{0,2},{1,3},{2,0},{3,1},{4,6},{5,7},{6,4},{7,5},{8,10},{9,11},{10,... | collective-permute-start | bytes 196616 | tf_op jit(solution)/shard_map/ppermute | solution.py:358
  89.3 2.0 %collective-permute-start.19 = (f32[136,128]{1,0:T(8,128)S(1)}, f32[136,128]{1,0:T(8,128)S(1)}, u32[]{:S(2)}, u32[]{:S(2)}) collective-permute-start(f32[136,128]{1,0:T(8,128)S(1)} %add.24.one_ref), channel_id=1, source_target_pairs={{0,2},{1,3},{2,0},{3,1},{4,6},{5,7},{6,4},{7,5},{8,10},{9,11},{10,... | collective-permute-start | bytes 208904 | tf_op jit(solution)/shard_map/ppermute | solution.py:358
  93.7 2.0 %collective-permute-start.20 = (f32[136,128]{1,0:T(8,128)S(1)}, f32[136,128]{1,0:T(8,128)S(1)}, u32[]{:S(2)}, u32[]{:S(2)}) collective-permute-start(f32[136,128]{1,0:T(8,128)S(1)} %add.25.front), channel_id=1, source_target_pairs={{0,4},{1,5},{2,6},{3,7},{4,0},{5,1},{6,2},{7,3},{8,12},{9,13},{10,... | collective-permute-start | bytes 208904 | tf_op jit(solution)/shard_map/ppermute | solution.py:358
  95.7 2.0 %collective-permute-start.23 = (f32[128,128]{1,0:T(8,128)S(1)}, f32[128,128]{1,0:T(8,128)S(1)}, u32[]{:S(2)}, u32[]{:S(2)}) collective-permute-start(f32[128,128]{1,0:T(8,128)S(1)} %add.27.back), channel_id=1, source_target_pairs={{0,4},{1,5},{2,6},{3,7},{4,0},{5,1},{6,2},{7,3},{8,12},{9,13},{10,... | collective-permute-start | bytes 196616 | tf_op jit(solution)/shard_map/ppermute | solution.py:358
  97.7 3.3 %collective-permute-done.23.back_last = f32[128,128]{1,0:T(8,128)S(1)} collective-permute-done((f32[128,128]{1,0:T(8,128)S(1)}, f32[128,128]{1,0:T(8,128)S(1)}, u32[]{:S(2)}, u32[]{:S(2)}) %collective-permute-start.23) | collective-permute-done | bytes 65568 | tf_op jit(solution)/shard_map/ppermute | solution.py:358
  101.3 2.1 %own.5.partial_ref = f32[32,4096]{1,0:T(8,128)S(1)} custom-call(f32[32,1024]{1,0:T(8,128)S(1)} %get-tuple-element.72.clipped_ref, bf16[2048,4096]{1,0:T(8,128)(2,1)S(1)} %get-tuple-element.53.high_ref, f8e4m3fn[2048,4096]{1,0:T(32,128)(4,1)S(1)} %get-tuple-element.54.low_ref), custom_call_target="tpu_custom_call" | custom-call | tf_op jit(solution)/shard_map/own/pallas_call | solution.py:326
  104.1 5.7 %rest.5 = (f32[32,4096]{1,0:T(8,128)S(1)}, bf16[64,4096]{1,0:T(8,128)(2,1)S(1)}, f8e4m3fn[32,4096]{1,0:T(32,128)(4,1)S(1)}, f32[264,128]{1,0:T(8,128)S(1)}, f32[40,128]{1,0:T(8,128)S(1)}) custom-call(f32[32,1024]{1,0:T(8,128)S(1)} %collective-permute-done.24.clipped_ref, bf16[2048,4096]{1,0:T(8,128)(2,1)S(1)} %get-tuple-element.53.high_ref, ...), custom_call_target="tpu_custom_call" | custom-call | tf_op jit(solution)/shard_map/rest/pallas_call | solution.py:326
  110.4 3.4 %image.5.own_ref = f32[264,128]{1,0:T(8,128)S(1)} custom-call(bf16[64,4096]{1,0:T(8,128)(2,1)S(1)} %get-tuple-element.73.pair_ref, f8e4m3fn[32,4096]{1,0:T(32,128)(4,1)S(1)} %get-tuple-element.74.coarse_ref, f32[40,128]{1,0:T(8,128)S(1)} %get-tuple-element.75.notes_ref, bf16[2048,4096]{1,0:T(8,128)(2,1)S(1)} %get-tuple-element.53.high_ref, ...), custom_call_target="tpu_custom_call" | custom-call | tf_op jit(solution)/shard_map/image/pallas_call | solution.py:326
  118.2 2.0 %collective-permute-start.27 = (f32[136,128]{1,0:T(8,128)S(1)}, f32[136,128]{1,0:T(8,128)S(1)}, u32[]{:S(2)}, u32[]{:S(2)}) collective-permute-start(f32[136,128]{1,0:T(8,128)S(1)} %add.28.one_ref), channel_id=1, source_target_pairs={{0,2},{1,3},{2,0},{3,1},{4,6},{5,7},{6,4},{7,5},{8,10},{9,11},{10,... | collective-permute-start | bytes 208904 | tf_op jit(solution)/shard_map/ppermute | solution.py:358
  122.6 2.0 %collective-permute-start.28 = (f32[136,128]{1,0:T(8,128)S(1)}, f32[136,128]{1,0:T(8,128)S(1)}, u32[]{:S(2)}, u32[]{:S(2)}) collective-permute-start(f32[136,128]{1,0:T(8,128)S(1)} %add.29.front), channel_id=1, source_target_pairs={{0,4},{1,5},{2,6},{3,7},{4,0},{5,1},{6,2},{7,3},{8,12},{9,13},{10,... | collective-permute-start | bytes 208904 | tf_op jit(solution)/shard_map/ppermute | solution.py:358
  126.2 3.7 %collective-permute-done.31.back_last = f32[128,128]{1,0:T(8,128)S(1)} collective-permute-done((f32[128,128]{1,0:T(8,128)S(1)}, f32[128,128]{1,0:T(8,128)S(1)}, u32[]{:S(2)}, u32[]{:S(2)}) %collective-permute-start.31) | collective-permute-done | bytes 65568 | tf_op jit(solution)/shard_map/ppermute | solution.py:358
  (78 shorter events, 26.5 us)
Async XLA Ops:
  0.6 2.7 %collective-permute-start = (s32[1024,128]{1,0:T(8,128)}, s32[1024,128]{1,0:T(8,128)S(1)}, u32[]{:S(2)}, u32[]{:S(2)}) collective-permute-start(s32[1024,128]{1,0:T(8,128)} %own_ref.1), channel_id=1, source_target_pairs={{0,8},{8,0},{1,9},{9,1},{2,10},{10,2},{3,11},{11,3},{4,12},{12,4},... | collective-permute-start | bytes 1572872 | tf_op jit(solution)/shard_map/ppermute | solution.py:348
  26.9 5.3 %collective-permute-start.2 = (f32[128,128]{1,0:T(8,128)S(1)}, f32[128,128]{1,0:T(8,128)S(1)}, u32[]{:S(2)}, u32[]{:S(2)}) collective-permute-start(f32[128,128]{1,0:T(8,128)S(1)} %get-tuple-element.50.one_ref), channel_id=1, source_target_pairs={{0,1},{1,0},{2,3},{3,2},{4,5},{5,4},{6,7},{7,6},{8,9},{9,8},{10,11... | collective-permute-start | bytes 196616 | tf_op jit(solution)/shard_map/ppermute | solution.py:358
  29.6 4.5 %collective-permute-start.5 = (f32[128,128]{1,0:T(8,128)S(1)}, f32[128,128]{1,0:T(8,128)S(1)}, u32[]{:S(2)}, u32[]{:S(2)}) collective-permute-start(f32[128,128]{1,0:T(8,128)S(1)} %get-tuple-element.51.one_ref), channel_id=1, source_target_pairs={{0,2},{1,3},{2,0},{3,1},{4,6},{5,7},{6,4},{7,5},{8,10},{9,11},{10,... | collective-permute-start | bytes 196616 | tf_op jit(solution)/shard_map/ppermute | solution.py:358
  32.2 4.3 %collective-permute-start.3 = (f32[128,128]{1,0:T(8,128)S(1)}, f32[128,128]{1,0:T(8,128)S(1)}, u32[]{:S(2)}, u32[]{:S(2)}) collective-permute-start(f32[128,128]{1,0:T(8,128)S(1)} %add.16.one_ref), channel_id=1, source_target_pairs={{0,2},{1,3},{2,0},{3,1},{4,6},{5,7},{6,4},{7,5},{8,10},{9,11},{10,... | collective-permute-start | bytes 196616 | tf_op jit(solution)/shard_map/ppermute | solution.py:358
  34.1 5.3 %collective-permute-start.6 = (f32[128,128]{1,0:T(8,128)S(1)}, f32[128,128]{1,0:T(8,128)S(1)}, u32[]{:S(2)}, u32[]{:S(2)}) collective-permute-start(f32[128,128]{1,0:T(8,128)S(1)} %add.18.one_ref), channel_id=1, source_target_pairs={{0,1},{1,0},{2,3},{3,2},{4,5},{5,4},{6,7},{7,6},{8,9},{9,8},{10,11... | collective-permute-start | bytes 196616 | tf_op jit(solution)/shard_map/ppermute | solution.py:358
  36.6 7.3 %collective-permute-start.4 = (f32[128,128]{1,0:T(8,128)S(1)}, f32[128,128]{1,0:T(8,128)S(1)}, u32[]{:S(2)}, u32[]{:S(2)}) collective-permute-start(f32[128,128]{1,0:T(8,128)S(1)} %add.17.front), channel_id=1, source_target_pairs={{0,4},{1,5},{2,6},{3,7},{4,0},{5,1},{6,2},{7,3},{8,12},{9,13},{10,... | collective-permute-start | bytes 196616 | tf_op jit(solution)/shard_map/ppermute | solution.py:358
  39.5 5.2 %collective-permute-start.7 = (f32[128,128]{1,0:T(8,128)S(1)}, f32[128,128]{1,0:T(8,128)S(1)}, u32[]{:S(2)}, u32[]{:S(2)}) collective-permute-start(f32[128,128]{1,0:T(8,128)S(1)} %add.19.back), channel_id=1, source_target_pairs={{0,4},{1,5},{2,6},{3,7},{4,0},{5,1},{6,2},{7,3},{8,12},{9,13},{10,... | collective-permute-start | bytes 196616 | tf_op jit(solution)/shard_map/ppermute | solution.py:358
  44.7 2.2 %collective-permute-start.8 = (f32[32,1024]{1,0:T(8,128)S(1)}, f32[32,1024]{1,0:T(8,128)S(1)}, u32[]{:S(2)}, u32[]{:S(2)}) collective-permute-start(f32[32,1024]{1,0:T(8,128)S(1)} %get-tuple-element.52.clipped_ref), channel_id=1, source_target_pairs={{0,8},{8,0},{1,9},{9,1},{2,10},{10,2},{3,11},{11,3},{4,12},{12,4},... | collective-permute-start | bytes 393224 | tf_op jit(solution)/shard_map/ppermute | solution.py:348
  52.6 4.0 %collective-permute-start.9 = (f32[264,128]{1,0:T(8,128)S(1)}, f32[264,128]{1,0:T(8,128)S(1)}, u32[]{:S(2)}, u32[]{:S(2)}) collective-permute-start(f32[264,128]{1,0:T(8,128)S(1)} %get-tuple-element.59), channel_id=1, source_target_pairs={{0,8},{8,0},{1,9},{9,1},{2,10},{10,2},{3,11},{11,3},{4,12},{12,4},... | collective-permute-start | bytes 405512 | tf_op jit(solution)/shard_map/ppermute | solution.py:348
  56.7 4.4 %collective-permute-start.10 = (f32[136,128]{1,0:T(8,128)S(1)}, f32[136,128]{1,0:T(8,128)S(1)}, u32[]{:S(2)}, u32[]{:S(2)}) collective-permute-start(f32[136,128]{1,0:T(8,128)S(1)} %get-tuple-element.60.one_ref), channel_id=1, source_target_pairs={{0,1},{1,0},{2,3},{3,2},{4,5},{5,4},{6,7},{7,6},{8,9},{9,8},{10,11... | collective-permute-start | bytes 208904 | tf_op jit(solution)/shard_map/ppermute | solution.py:358
  58.3 4.4 %collective-permute-start.13 = (f32[128,128]{1,0:T(8,128)S(1)}, f32[128,128]{1,0:T(8,128)S(1)}, u32[]{:S(2)}, u32[]{:S(2)}) collective-permute-start(f32[128,128]{1,0:T(8,128)S(1)} %get-tuple-element.61.one_ref), channel_id=1, source_target_pairs={{0,2},{1,3},{2,0},{3,1},{4,6},{5,7},{6,4},{7,5},{8,10},{9,11},{10,... | collective-permute-start | bytes 196616 | tf_op jit(solution)/shard_map/ppermute | solution.py:358
  61.1 4.4 %collective-permute-start.11 = (f32[136,128]{1,0:T(8,128)S(1)}, f32[136,128]{1,0:T(8,128)S(1)}, u32[]{:S(2)}, u32[]{:S(2)}) collective-permute-start(f32[136,128]{1,0:T(8,128)S(1)} %add.20.one_ref), channel_id=1, source_target_pairs={{0,2},{1,3},{2,0},{3,1},{4,6},{5,7},{6,4},{7,5},{8,10},{9,11},{10,... | collective-permute-start | bytes 208904 | tf_op jit(solution)/shard_map/ppermute | solution.py:358
  62.7 4.5 %collective-permute-start.14 = (f32[128,128]{1,0:T(8,128)S(1)}, f32[128,128]{1,0:T(8,128)S(1)}, u32[]{:S(2)}, u32[]{:S(2)}) collective-permute-start(f32[128,128]{1,0:T(8,128)S(1)} %add.22.one_ref), channel_id=1, source_target_pairs={{0,1},{1,0},{2,3},{3,2},{4,5},{5,4},{6,7},{7,6},{8,9},{9,8},{10,11... | collective-permute-start | bytes 196616 | tf_op jit(solution)/shard_map/ppermute | solution.py:358
  65.5 7.1 %collective-permute-start.12 = (f32[136,128]{1,0:T(8,128)S(1)}, f32[136,128]{1,0:T(8,128)S(1)}, u32[]{:S(2)}, u32[]{:S(2)}) collective-permute-start(f32[136,128]{1,0:T(8,128)S(1)} %add.21.front), channel_id=1, source_target_pairs={{0,4},{1,5},{2,6},{3,7},{4,0},{5,1},{6,2},{7,3},{8,12},{9,13},{10,... | collective-permute-start | bytes 208904 | tf_op jit(solution)/shard_map/ppermute | solution.py:358
  67.2 5.3 %collective-permute-start.15 = (f32[128,128]{1,0:T(8,128)S(1)}, f32[128,128]{1,0:T(8,128)S(1)}, u32[]{:S(2)}, u32[]{:S(2)}) collective-permute-start(f32[128,128]{1,0:T(8,128)S(1)} %add.23.back), channel_id=1, source_target_pairs={{0,4},{1,5},{2,6},{3,7},{4,0},{5,1},{6,2},{7,3},{8,12},{9,13},{10,... | collective-permute-start | bytes 196616 | tf_op jit(solution)/shard_map/ppermute | solution.py:358
  80.9 4.0 %collective-permute-start.17 = (f32[264,128]{1,0:T(8,128)S(1)}, f32[264,128]{1,0:T(8,128)S(1)}, u32[]{:S(2)}, u32[]{:S(2)}) collective-permute-start(f32[264,128]{1,0:T(8,128)S(1)} %get-tuple-element.67), channel_id=1, source_target_pairs={{0,8},{8,0},{1,9},{9,1},{2,10},{10,2},{3,11},{11,3},{4,12},{12,4},... | collective-permute-start | bytes 405512 | tf_op jit(solution)/shard_map/ppermute | solution.py:348
  84.9 4.4 %collective-permute-start.18 = (f32[136,128]{1,0:T(8,128)S(1)}, f32[136,128]{1,0:T(8,128)S(1)}, u32[]{:S(2)}, u32[]{:S(2)}) collective-permute-start(f32[136,128]{1,0:T(8,128)S(1)} %get-tuple-element.68.one_ref), channel_id=1, source_target_pairs={{0,1},{1,0},{2,3},{3,2},{4,5},{5,4},{6,7},{7,6},{8,9},{9,8},{10,11... | collective-permute-start | bytes 208904 | tf_op jit(solution)/shard_map/ppermute | solution.py:358
  86.5 4.8 %collective-permute-start.21 = (f32[128,128]{1,0:T(8,128)S(1)}, f32[128,128]{1,0:T(8,128)S(1)}, u32[]{:S(2)}, u32[]{:S(2)}) collective-permute-start(f32[128,128]{1,0:T(8,128)S(1)} %get-tuple-element.69.one_ref), channel_id=1, source_target_pairs={{0,2},{1,3},{2,0},{3,1},{4,6},{5,7},{6,4},{7,5},{8,10},{9,11},{10,... | collective-permute-start | bytes 196616 | tf_op jit(solution)/shard_map/ppermute | solution.py:358
  89.3 4.4 %collective-permute-start.19 = (f32[136,128]{1,0:T(8,128)S(1)}, f32[136,128]{1,0:T(8,128)S(1)}, u32[]{:S(2)}, u32[]{:S(2)}) collective-permute-start(f32[136,128]{1,0:T(8,128)S(1)} %add.24.one_ref), channel_id=1, source_target_pairs={{0,2},{1,3},{2,0},{3,1},{4,6},{5,7},{6,4},{7,5},{8,10},{9,11},{10,... | collective-permute-start | bytes 208904 | tf_op jit(solution)/shard_map/ppermute | solution.py:358
  91.3 4.4 %collective-permute-start.22 = (f32[128,128]{1,0:T(8,128)S(1)}, f32[128,128]{1,0:T(8,128)S(1)}, u32[]{:S(2)}, u32[]{:S(2)}) collective-permute-start(f32[128,128]{1,0:T(8,128)S(1)} %add.26.one_ref), channel_id=1, source_target_pairs={{0,1},{1,0},{2,3},{3,2},{4,5},{5,4},{6,7},{7,6},{8,9},{9,8},{10,11... | collective-permute-start | bytes 196616 | tf_op jit(solution)/shard_map/ppermute | solution.py:358
  93.7 7.4 %collective-permute-start.20 = (f32[136,128]{1,0:T(8,128)S(1)}, f32[136,128]{1,0:T(8,128)S(1)}, u32[]{:S(2)}, u32[]{:S(2)}) collective-permute-start(f32[136,128]{1,0:T(8,128)S(1)} %add.25.front), channel_id=1, source_target_pairs={{0,4},{1,5},{2,6},{3,7},{4,0},{5,1},{6,2},{7,3},{8,12},{9,13},{10,... | collective-permute-start | bytes 208904 | tf_op jit(solution)/shard_map/ppermute | solution.py:358
  95.7 5.3 %collective-permute-start.23 = (f32[128,128]{1,0:T(8,128)S(1)}, f32[128,128]{1,0:T(8,128)S(1)}, u32[]{:S(2)}, u32[]{:S(2)}) collective-permute-start(f32[128,128]{1,0:T(8,128)S(1)} %add.27.back), channel_id=1, source_target_pairs={{0,4},{1,5},{2,6},{3,7},{4,0},{5,1},{6,2},{7,3},{8,12},{9,13},{10,... | collective-permute-start | bytes 196616 | tf_op jit(solution)/shard_map/ppermute | solution.py:358
  101.2 2.9 %collective-permute-start.24 = (f32[32,1024]{1,0:T(8,128)S(1)}, f32[32,1024]{1,0:T(8,128)S(1)}, u32[]{:S(2)}, u32[]{:S(2)}) collective-permute-start(f32[32,1024]{1,0:T(8,128)S(1)} %get-tuple-element.72.clipped_ref), channel_id=1, source_target_pairs={{0,8},{8,0},{1,9},{9,1},{2,10},{10,2},{3,11},{11,3},{4,12},{12,4},... | collective-permute-start | bytes 393224 | tf_op jit(solution)/shard_map/ppermute | solution.py:348
  103.6 26.4 %collective-permute-start.32 = (f32[32,4096]{1,0:T(8,128)S(1)}, f32[32,4096]{1,0:T(8,128)S(1)}, u32[]{:S(2)}, u32[]{:S(2)}) collective-permute-start(f32[32,4096]{1,0:T(8,128)S(1)} %sum.1.refs_1_), channel_id=1, source_target_pairs={{0,8},{8,0},{1,9},{9,1},{2,10},{10,2},{3,11},{11,3},{4,12},{12,4},... | collective-permute-start | bytes 1572872 | tf_op jit(solution)/shard_map/ppermute | solution.py:348
  109.8 20.1 %collective-permute-start.33 = (f32[32,4096]{1,0:T(8,128)S(1)}, f32[32,4096]{1,0:T(8,128)S(1)}, u32[]{:S(2)}, u32[]{:S(2)}) collective-permute-start(f32[32,4096]{1,0:T(8,128)S(1)} %get-tuple-element.85.refs_3_), channel_id=1, source_target_pairs={{0,8},{8,0},{1,9},{9,1},{2,10},{10,2},{3,11},{11,3},{4,12},{12,4},... | collective-permute-start | bytes 1572872 | tf_op jit(solution)/shard_map/ppermute | solution.py:348
  109.9 3.9 %collective-permute-start.25 = (f32[264,128]{1,0:T(8,128)S(1)}, f32[264,128]{1,0:T(8,128)S(1)}, u32[]{:S(2)}, u32[]{:S(2)}) collective-permute-start(f32[264,128]{1,0:T(8,128)S(1)} %get-tuple-element.76), channel_id=1, source_target_pairs={{0,8},{8,0},{1,9},{9,1},{2,10},{10,2},{3,11},{11,3},{4,12},{12,4},... | collective-permute-start | bytes 405512 | tf_op jit(solution)/shard_map/ppermute | solution.py:348
  113.8 4.4 %collective-permute-start.26 = (f32[136,128]{1,0:T(8,128)S(1)}, f32[136,128]{1,0:T(8,128)S(1)}, u32[]{:S(2)}, u32[]{:S(2)}) collective-permute-start(f32[136,128]{1,0:T(8,128)S(1)} %get-tuple-element.77.one_ref), channel_id=1, source_target_pairs={{0,1},{1,0},{2,3},{3,2},{4,5},{5,4},{6,7},{7,6},{8,9},{9,8},{10,11... | collective-permute-start | bytes 208904 | tf_op jit(solution)/shard_map/ppermute | solution.py:358
  115.4 4.8 %collective-permute-start.29 = (f32[128,128]{1,0:T(8,128)S(1)}, f32[128,128]{1,0:T(8,128)S(1)}, u32[]{:S(2)}, u32[]{:S(2)}) collective-permute-start(f32[128,128]{1,0:T(8,128)S(1)} %get-tuple-element.78.one_ref), channel_id=1, source_target_pairs={{0,2},{1,3},{2,0},{3,1},{4,6},{5,7},{6,4},{7,5},{8,10},{9,11},{10,... | collective-permute-start | bytes 196616 | tf_op jit(solution)/shard_map/ppermute | solution.py:358
  118.2 4.4 %collective-permute-start.27 = (f32[136,128]{1,0:T(8,128)S(1)}, f32[136,128]{1,0:T(8,128)S(1)}, u32[]{:S(2)}, u32[]{:S(2)}) collective-permute-start(f32[136,128]{1,0:T(8,128)S(1)} %add.28.one_ref), channel_id=1, source_target_pairs={{0,2},{1,3},{2,0},{3,1},{4,6},{5,7},{6,4},{7,5},{8,10},{9,11},{10,... | collective-permute-start | bytes 208904 | tf_op jit(solution)/shard_map/ppermute | solution.py:358
  120.2 4.4 %collective-permute-start.30 = (f32[128,128]{1,0:T(8,128)S(1)}, f32[128,128]{1,0:T(8,128)S(1)}, u32[]{:S(2)}, u32[]{:S(2)}) collective-permute-start(f32[128,128]{1,0:T(8,128)S(1)} %add.30.one_ref), channel_id=1, source_target_pairs={{0,1},{1,0},{2,3},{3,2},{4,5},{5,4},{6,7},{7,6},{8,9},{9,8},{10,11... | collective-permute-start | bytes 196616 | tf_op jit(solution)/shard_map/ppermute | solution.py:358
  122.6 7.3 %collective-permute-start.28 = (f32[136,128]{1,0:T(8,128)S(1)}, f32[136,128]{1,0:T(8,128)S(1)}, u32[]{:S(2)}, u32[]{:S(2)}) collective-permute-start(f32[136,128]{1,0:T(8,128)S(1)} %add.29.front), channel_id=1, source_target_pairs={{0,4},{1,5},{2,6},{3,7},{4,0},{5,1},{6,2},{7,3},{8,12},{9,13},{10,... | collective-permute-start | bytes 208904 | tf_op jit(solution)/shard_map/ppermute | solution.py:358
  124.7 5.3 %collective-permute-start.31 = (f32[128,128]{1,0:T(8,128)S(1)}, f32[128,128]{1,0:T(8,128)S(1)}, u32[]{:S(2)}, u32[]{:S(2)}) collective-permute-start(f32[128,128]{1,0:T(8,128)S(1)} %add.31.back), channel_id=1, source_target_pairs={{0,4},{1,5},{2,6},{3,7},{4,0},{5,1},{6,2},{7,3},{8,12},{9,13},{10,... | collective-permute-start | bytes 196616 | tf_op jit(solution)/shard_map/ppermute | solution.py:358
  (4 other events, 64.6 us)

commit v2 on v1

--- a/solution.py
+++ b/solution.py
@@ -190,7 +190,7 @@
 
 def own_kernel(clipped_ref, high_ref, low_ref, partial_out):
     paths, width = high_ref.shape
-    cols = divisor(width, 1024)
+    cols = divisor(width, 4096)
     for index in range(width // cols):
         span = pl.ds(index * cols, cols)
         partial_out[:, span] = gradient_of(clipped_ref[...], high_ref, low_ref, pl.ds(0, paths // 2), span)
@@ -202,7 +202,7 @@
     paths, width = high_ref.shape
     half = paths // 2
     count = clipped_ref.shape[0]
-    cols = divisor(width, 1024)
+    cols = divisor(width, 4096)
     squares = jnp.zeros((8, 128), f32)
     largest = jnp.zeros((count, 128), f32)
     for index in range(width // cols):

time: 132 us -> 131 us (level)
  no operation moved by 1% of the time
where the time goes in v2:
time: 131 us
  Pallas kernels  60.1 us (46%)
  starting transfers between devices  46.3 us (35%)
  waiting for transfers between devices  23.9 us (18%)
    pallas_call x36, Pallas kernels, call(): pl.pallas_call(kernel, out_shape=shapes, in_specs=specs or vmem(len(argum...  60.1 us
    ppermute x24, starting transfers between devices, all_chips(): lax.ppermute(array, 'feats', [(chip, chip ^ order[step]) for chip in rang...  43.2 us
    ppermute x24, waiting for transfers between devices, all_chips(): lax.ppermute(array, 'feats', [(chip, chip ^ order[step]) for chip in rang...  22.6 us
    ppermute x10, starting transfers between devices, swap(): return lax.ppermute(array, 'paths', [(0, 1), (1, 0)])  3.13 us
  transfers between devices with their start and end apart: 34, of which 14 were waited for; matrix products, arithmetic and copies ran while one was open for 0% of the time, Pallas kernels for 19%

profile of v2, /device:TPU:0, one launch (start us, length us, event | category | flops | bytes accessed | tf_op | source)
XLA Modules:
  0.0 131.2 jit_solution(5851356246550331076)
XLA Ops:
  1.1 2.1 %prepare.1 = (bf16[1024,256]{1,0:T(8,128)(2,1)S(1)}, bf16[256,4096]{1,0:T(8,128)(2,1)S(1)}, bf16[64,4096]{1,0:T(8,128)(2,1)S(1)}, f32[1,4096]{1,0:T(1,128)S(1)}) custom-call(s32[1024,128]{1,0:T(8,128)} %own_ref.1, s32[128,8192]{1,0:T(8,128)} %freq_ref.1, s32[1,8192]{1,0:T(1,128)} %bitcast.2, f32[1,8192]{1,0:T(1,128)} %bitcast.3, f32[32,8192]{1,0:T(8,128)} %refs_0_.1), custom_call_target="tpu_custom_call" | custom-call | tf_op jit(solution)/shard_map/prepare/pallas_call | solution.py:326
  3.3 22.1 %build.1 = (f32[32,1024]{1,0:T(8,128)S(1)}, f32[32,1024]{1,0:T(8,128)S(1)}, bf16[2048,4096]{1,0:T(8,128)(2,1)S(1)}, f8e4m3fn[2048,4096]{1,0:T(32,128)(4,1)S(1)}) custom-call(bf16[1024,256]{1,0:T(8,128)(2,1)S(1)} %get-tuple-element.45.own_ref, s32[1024,128]{1,0:T(8,128)S(1)} %collective-permute-done.other_ref, ...), custom_call_target="tpu_custom_call", output_to_operand_aliasing={{2}: (4, {}), {3}: (5, {})} | custom-call | tf_op jit(solution)/shard_map/build/pallas_call | solution.py:326
  26.9 2.7 %collective-permute-start.2 = (f32[128,128]{1,0:T(8,128)S(1)}, f32[128,128]{1,0:T(8,128)S(1)}, u32[]{:S(2)}, u32[]{:S(2)}) collective-permute-start(f32[128,128]{1,0:T(8,128)S(1)} %get-tuple-element.50.one_ref), channel_id=1, source_target_pairs={{0,1},{1,0},{2,3},{3,2},{4,5},{5,4},{6,7},{7,6},{8,9},{9,8},{10,11... | collective-permute-start | bytes 196616 | tf_op jit(solution)/shard_map/ppermute | solution.py:358
  32.2 1.9 %collective-permute-start.3 = (f32[128,128]{1,0:T(8,128)S(1)}, f32[128,128]{1,0:T(8,128)S(1)}, u32[]{:S(2)}, u32[]{:S(2)}) collective-permute-start(f32[128,128]{1,0:T(8,128)S(1)} %add.16.one_ref), channel_id=1, source_target_pairs={{0,2},{1,3},{2,0},{3,1},{4,6},{5,7},{6,4},{7,5},{8,10},{9,11},{10,... | collective-permute-start | bytes 196616 | tf_op jit(solution)/shard_map/ppermute | solution.py:358
  34.1 1.6 %collective-permute-start.6 = (f32[128,128]{1,0:T(8,128)S(1)}, f32[128,128]{1,0:T(8,128)S(1)}, u32[]{:S(2)}, u32[]{:S(2)}) collective-permute-start(f32[128,128]{1,0:T(8,128)S(1)} %add.18.one_ref), channel_id=1, source_target_pairs={{0,1},{1,0},{2,3},{3,2},{4,5},{5,4},{6,7},{7,6},{8,9},{9,8},{10,11... | collective-permute-start | bytes 196616 | tf_op jit(solution)/shard_map/ppermute | solution.py:358
  36.6 2.9 %collective-permute-start.4 = (f32[128,128]{1,0:T(8,128)S(1)}, f32[128,128]{1,0:T(8,128)S(1)}, u32[]{:S(2)}, u32[]{:S(2)}) collective-permute-start(f32[128,128]{1,0:T(8,128)S(1)} %add.17.front), channel_id=1, source_target_pairs={{0,4},{1,5},{2,6},{3,7},{4,0},{5,1},{6,2},{7,3},{8,12},{9,13},{10,... | collective-permute-start | bytes 196616 | tf_op jit(solution)/shard_map/ppermute | solution.py:358
  39.5 1.6 %collective-permute-start.7 = (f32[128,128]{1,0:T(8,128)S(1)}, f32[128,128]{1,0:T(8,128)S(1)}, u32[]{:S(2)}, u32[]{:S(2)}) collective-permute-start(f32[128,128]{1,0:T(8,128)S(1)} %add.19.back), channel_id=1, source_target_pairs={{0,4},{1,5},{2,6},{3,7},{4,0},{5,1},{6,2},{7,3},{8,12},{9,13},{10,... | collective-permute-start | bytes 196616 | tf_op jit(solution)/shard_map/ppermute | solution.py:358
  41.1 2.8 %collective-permute-done.4.front_last = f32[128,128]{1,0:T(8,128)S(1)} collective-permute-done((f32[128,128]{1,0:T(8,128)S(1)}, f32[128,128]{1,0:T(8,128)S(1)}, u32[]{:S(2)}, u32[]{:S(2)}) %collective-permute-start.4) | collective-permute-done | bytes 65568 | tf_op jit(solution)/shard_map/ppermute | solution.py:358
  44.8 2.1 %own.3.partial_ref = f32[32,4096]{1,0:T(8,128)S(1)} custom-call(f32[32,1024]{1,0:T(8,128)S(1)} %get-tuple-element.52.clipped_ref, bf16[2048,4096]{1,0:T(8,128)(2,1)S(1)} %get-tuple-element.53.high_ref, f8e4m3fn[2048,4096]{1,0:T(32,128)(4,1)S(1)} %get-tuple-element.54.low_ref), custom_call_target="tpu_custom_call" | custom-call | tf_op jit(solution)/shard_map/own/pallas_call | solution.py:326
  46.9 5.7 %rest.3 = (f32[32,4096]{1,0:T(8,128)S(1)}, bf16[64,4096]{1,0:T(8,128)(2,1)S(1)}, f8e4m3fn[32,4096]{1,0:T(32,128)(4,1)S(1)}, f32[264,128]{1,0:T(8,128)S(1)}, f32[40,128]{1,0:T(8,128)S(1)}) custom-call(f32[32,1024]{1,0:T(8,128)S(1)} %collective-permute-done.8.clipped_ref, bf16[2048,4096]{1,0:T(8,128)(2,1)S(1)} %get-tuple-element.53.high_ref, ...), custom_call_target="tpu_custom_call" | custom-call | tf_op jit(solution)/shard_map/rest/pallas_call | solution.py:326
  53.1 3.4 %image.3.own_ref = f32[264,128]{1,0:T(8,128)S(1)} custom-call(bf16[64,4096]{1,0:T(8,128)(2,1)S(1)} %get-tuple-element.56.pair_ref, f8e4m3fn[32,4096]{1,0:T(32,128)(4,1)S(1)} %get-tuple-element.57.coarse_ref, f32[40,128]{1,0:T(8,128)S(1)} %get-tuple-element.58.notes_ref, bf16[2048,4096]{1,0:T(8,128)(2,1)S(1)} %get-tuple-element.53.high_ref, ...), custom_call_target="tpu_custom_call" | custom-call | tf_op jit(solution)/shard_map/image/pallas_call | solution.py:326
  56.6 1.6 %collective-permute-start.10 = (f32[136,128]{1,0:T(8,128)S(1)}, f32[136,128]{1,0:T(8,128)S(1)}, u32[]{:S(2)}, u32[]{:S(2)}) collective-permute-start(f32[136,128]{1,0:T(8,128)S(1)} %get-tuple-element.60.one_ref), channel_id=1, source_target_pairs={{0,1},{1,0},{2,3},{3,2},{4,5},{5,4},{6,7},{7,6},{8,9},{9,8},{10,11... | collective-permute-start | bytes 208904 | tf_op jit(solution)/shard_map/ppermute | solution.py:358
  61.0 1.6 %collective-permute-start.11 = (f32[136,128]{1,0:T(8,128)S(1)}, f32[136,128]{1,0:T(8,128)S(1)}, u32[]{:S(2)}, u32[]{:S(2)}) collective-permute-start(f32[136,128]{1,0:T(8,128)S(1)} %add.20.one_ref), channel_id=1, source_target_pairs={{0,2},{1,3},{2,0},{3,1},{4,6},{5,7},{6,4},{7,5},{8,10},{9,11},{10,... | collective-permute-start | bytes 208904 | tf_op jit(solution)/shard_map/ppermute | solution.py:358
  62.7 1.6 %collective-permute-start.14 = (f32[128,128]{1,0:T(8,128)S(1)}, f32[128,128]{1,0:T(8,128)S(1)}, u32[]{:S(2)}, u32[]{:S(2)}) collective-permute-start(f32[128,128]{1,0:T(8,128)S(1)} %add.22.one_ref), channel_id=1, source_target_pairs={{0,1},{1,0},{2,3},{3,2},{4,5},{5,4},{6,7},{7,6},{8,9},{9,8},{10,11... | collective-permute-start | bytes 196616 | tf_op jit(solution)/shard_map/ppermute | solution.py:358
  65.4 1.8 %collective-permute-start.12 = (f32[136,128]{1,0:T(8,128)S(1)}, f32[136,128]{1,0:T(8,128)S(1)}, u32[]{:S(2)}, u32[]{:S(2)}) collective-permute-start(f32[136,128]{1,0:T(8,128)S(1)} %add.21.front), channel_id=1, source_target_pairs={{0,4},{1,5},{2,6},{3,7},{4,0},{5,1},{6,2},{7,3},{8,12},{9,13},{10,... | collective-permute-start | bytes 208904 | tf_op jit(solution)/shard_map/ppermute | solution.py:358
  67.2 2.0 %collective-permute-start.15 = (f32[128,128]{1,0:T(8,128)S(1)}, f32[128,128]{1,0:T(8,128)S(1)}, u32[]{:S(2)}, u32[]{:S(2)}) collective-permute-start(f32[128,128]{1,0:T(8,128)S(1)} %add.23.back), channel_id=1, source_target_pairs={{0,4},{1,5},{2,6},{3,7},{4,0},{5,1},{6,2},{7,3},{8,12},{9,13},{10,... | collective-permute-start | bytes 196616 | tf_op jit(solution)/shard_map/ppermute | solution.py:358
  69.2 3.3 %collective-permute-done.15.back_last = f32[128,128]{1,0:T(8,128)S(1)} collective-permute-done((f32[128,128]{1,0:T(8,128)S(1)}, f32[128,128]{1,0:T(8,128)S(1)}, u32[]{:S(2)}, u32[]{:S(2)}) %collective-permute-start.15) | collective-permute-done | bytes 65568 | tf_op jit(solution)/shard_map/ppermute | solution.py:358
  72.8 2.1 %own.4.partial_ref = f32[32,4096]{1,0:T(8,128)S(1)} custom-call(f32[32,1024]{1,0:T(8,128)S(1)} %get-tuple-element.63.clipped_ref, bf16[2048,4096]{1,0:T(8,128)(2,1)S(1)} %get-tuple-element.53.high_ref, f8e4m3fn[2048,4096]{1,0:T(32,128)(4,1)S(1)} %get-tuple-element.54.low_ref), custom_call_target="tpu_custom_call" | custom-call | tf_op jit(solution)/shard_map/own/pallas_call | solution.py:326
  74.9 5.9 %rest.4 = (f32[32,4096]{1,0:T(8,128)S(1)}, bf16[64,4096]{1,0:T(8,128)(2,1)S(1)}, f8e4m3fn[32,4096]{1,0:T(32,128)(4,1)S(1)}, f32[264,128]{1,0:T(8,128)S(1)}, f32[40,128]{1,0:T(8,128)S(1)}) custom-call(f32[32,1024]{1,0:T(8,128)S(1)} %collective-permute-done.16.clipped_ref, bf16[2048,4096]{1,0:T(8,128)(2,1)S(1)} %get-tuple-element.53.high_ref, ...), custom_call_target="tpu_custom_call" | custom-call | tf_op jit(solution)/shard_map/rest/pallas_call | solution.py:326
  81.3 3.4 %image.4.own_ref = f32[264,128]{1,0:T(8,128)S(1)} custom-call(bf16[64,4096]{1,0:T(8,128)(2,1)S(1)} %get-tuple-element.64.pair_ref, f8e4m3fn[32,4096]{1,0:T(32,128)(4,1)S(1)} %get-tuple-element.65.coarse_ref, f32[40,128]{1,0:T(8,128)S(1)} %get-tuple-element.66.notes_ref, bf16[2048,4096]{1,0:T(8,128)(2,1)S(1)} %get-tuple-element.53.high_ref, ...), custom_call_target="tpu_custom_call" | custom-call | tf_op jit(solution)/shard_map/image/pallas_call | solution.py:326
  84.8 1.6 %collective-permute-start.18 = (f32[136,128]{1,0:T(8,128)S(1)}, f32[136,128]{1,0:T(8,128)S(1)}, u32[]{:S(2)}, u32[]{:S(2)}) collective-permute-start(f32[136,128]{1,0:T(8,128)S(1)} %get-tuple-element.68.one_ref), channel_id=1, source_target_pairs={{0,1},{1,0},{2,3},{3,2},{4,5},{5,4},{6,7},{7,6},{8,9},{9,8},{10,11... | collective-permute-start | bytes 208904 | tf_op jit(solution)/shard_map/ppermute | solution.py:358
  86.4 1.9 %collective-permute-start.21 = (f32[128,128]{1,0:T(8,128)S(1)}, f32[128,128]{1,0:T(8,128)S(1)}, u32[]{:S(2)}, u32[]{:S(2)}) collective-permute-start(f32[128,128]{1,0:T(8,128)S(1)} %get-tuple-element.69.one_ref), channel_id=1, source_target_pairs={{0,2},{1,3},{2,0},{3,1},{4,6},{5,7},{6,4},{7,5},{8,10},{9,11},{10,... | collective-permute-start | bytes 196616 | tf_op jit(solution)/shard_map/ppermute | solution.py:358
  89.2 2.0 %collective-permute-start.19 = (f32[136,128]{1,0:T(8,128)S(1)}, f32[136,128]{1,0:T(8,128)S(1)}, u32[]{:S(2)}, u32[]{:S(2)}) collective-permute-start(f32[136,128]{1,0:T(8,128)S(1)} %add.24.one_ref), channel_id=1, source_target_pairs={{0,2},{1,3},{2,0},{3,1},{4,6},{5,7},{6,4},{7,5},{8,10},{9,11},{10,... | collective-permute-start | bytes 208904 | tf_op jit(solution)/shard_map/ppermute | solution.py:358
  93.5 2.0 %collective-permute-start.20 = (f32[136,128]{1,0:T(8,128)S(1)}, f32[136,128]{1,0:T(8,128)S(1)}, u32[]{:S(2)}, u32[]{:S(2)}) collective-permute-start(f32[136,128]{1,0:T(8,128)S(1)} %add.25.front), channel_id=1, source_target_pairs={{0,4},{1,5},{2,6},{3,7},{4,0},{5,1},{6,2},{7,3},{8,12},{9,13},{10,... | collective-permute-start | bytes 208904 | tf_op jit(solution)/shard_map/ppermute | solution.py:358
  95.6 2.0 %collective-permute-start.23 = (f32[128,128]{1,0:T(8,128)S(1)}, f32[128,128]{1,0:T(8,128)S(1)}, u32[]{:S(2)}, u32[]{:S(2)}) collective-permute-start(f32[128,128]{1,0:T(8,128)S(1)} %add.27.back), channel_id=1, source_target_pairs={{0,4},{1,5},{2,6},{3,7},{4,0},{5,1},{6,2},{7,3},{8,12},{9,13},{10,... | collective-permute-start | bytes 196616 | tf_op jit(solution)/shard_map/ppermute | solution.py:358
  97.6 3.3 %collective-permute-done.23.back_last = f32[128,128]{1,0:T(8,128)S(1)} collective-permute-done((f32[128,128]{1,0:T(8,128)S(1)}, f32[128,128]{1,0:T(8,128)S(1)}, u32[]{:S(2)}, u32[]{:S(2)}) %collective-permute-start.23) | collective-permute-done | bytes 65568 | tf_op jit(solution)/shard_map/ppermute | solution.py:358
  101.2 2.1 %own.5.partial_ref = f32[32,4096]{1,0:T(8,128)S(1)} custom-call(f32[32,1024]{1,0:T(8,128)S(1)} %get-tuple-element.72.clipped_ref, bf16[2048,4096]{1,0:T(8,128)(2,1)S(1)} %get-tuple-element.53.high_ref, f8e4m3fn[2048,4096]{1,0:T(32,128)(4,1)S(1)} %get-tuple-element.54.low_ref), custom_call_target="tpu_custom_call" | custom-call | tf_op jit(solution)/shard_map/own/pallas_call | solution.py:326
  104.0 5.6 %rest.5 = (f32[32,4096]{1,0:T(8,128)S(1)}, bf16[64,4096]{1,0:T(8,128)(2,1)S(1)}, f8e4m3fn[32,4096]{1,0:T(32,128)(4,1)S(1)}, f32[264,128]{1,0:T(8,128)S(1)}, f32[40,128]{1,0:T(8,128)S(1)}) custom-call(f32[32,1024]{1,0:T(8,128)S(1)} %collective-permute-done.24.clipped_ref, bf16[2048,4096]{1,0:T(8,128)(2,1)S(1)} %get-tuple-element.53.high_ref, ...), custom_call_target="tpu_custom_call" | custom-call | tf_op jit(solution)/shard_map/rest/pallas_call | solution.py:326
  110.2 3.4 %image.5.own_ref = f32[264,128]{1,0:T(8,128)S(1)} custom-call(bf16[64,4096]{1,0:T(8,128)(2,1)S(1)} %get-tuple-element.73.pair_ref, f8e4m3fn[32,4096]{1,0:T(32,128)(4,1)S(1)} %get-tuple-element.74.coarse_ref, f32[40,128]{1,0:T(8,128)S(1)} %get-tuple-element.75.notes_ref, bf16[2048,4096]{1,0:T(8,128)(2,1)S(1)} %get-tuple-element.53.high_ref, ...), custom_call_target="tpu_custom_call" | custom-call | tf_op jit(solution)/shard_map/image/pallas_call | solution.py:326
  118.1 2.0 %collective-permute-start.27 = (f32[136,128]{1,0:T(8,128)S(1)}, f32[136,128]{1,0:T(8,128)S(1)}, u32[]{:S(2)}, u32[]{:S(2)}) collective-permute-start(f32[136,128]{1,0:T(8,128)S(1)} %add.28.one_ref), channel_id=1, source_target_pairs={{0,2},{1,3},{2,0},{3,1},{4,6},{5,7},{6,4},{7,5},{8,10},{9,11},{10,... | collective-permute-start | bytes 208904 | tf_op jit(solution)/shard_map/ppermute | solution.py:358
  122.5 2.0 %collective-permute-start.28 = (f32[136,128]{1,0:T(8,128)S(1)}, f32[136,128]{1,0:T(8,128)S(1)}, u32[]{:S(2)}, u32[]{:S(2)}) collective-permute-start(f32[136,128]{1,0:T(8,128)S(1)} %add.29.front), channel_id=1, source_target_pairs={{0,4},{1,5},{2,6},{3,7},{4,0},{5,1},{6,2},{7,3},{8,12},{9,13},{10,... | collective-permute-start | bytes 208904 | tf_op jit(solution)/shard_map/ppermute | solution.py:358
  126.0 3.7 %collective-permute-done.31.back_last = f32[128,128]{1,0:T(8,128)S(1)} collective-permute-done((f32[128,128]{1,0:T(8,128)S(1)}, f32[128,128]{1,0:T(8,128)S(1)}, u32[]{:S(2)}, u32[]{:S(2)}) %collective-permute-start.31) | collective-permute-done | bytes 65568 | tf_op jit(solution)/shard_map/ppermute | solution.py:358
  (78 shorter events, 26.5 us)
Async XLA Ops:
  0.6 2.7 %collective-permute-start = (s32[1024,128]{1,0:T(8,128)}, s32[1024,128]{1,0:T(8,128)S(1)}, u32[]{:S(2)}, u32[]{:S(2)}) collective-permute-start(s32[1024,128]{1,0:T(8,128)} %own_ref.1), channel_id=1, source_target_pairs={{0,8},{8,0},{1,9},{9,1},{2,10},{10,2},{3,11},{11,3},{4,12},{12,4},... | collective-permute-start | bytes 1572872 | tf_op jit(solution)/shard_map/ppermute | solution.py:348
  26.9 5.3 %collective-permute-start.2 = (f32[128,128]{1,0:T(8,128)S(1)}, f32[128,128]{1,0:T(8,128)S(1)}, u32[]{:S(2)}, u32[]{:S(2)}) collective-permute-start(f32[128,128]{1,0:T(8,128)S(1)} %get-tuple-element.50.one_ref), channel_id=1, source_target_pairs={{0,1},{1,0},{2,3},{3,2},{4,5},{5,4},{6,7},{7,6},{8,9},{9,8},{10,11... | collective-permute-start | bytes 196616 | tf_op jit(solution)/shard_map/ppermute | solution.py:358
  29.6 4.5 %collective-permute-start.5 = (f32[128,128]{1,0:T(8,128)S(1)}, f32[128,128]{1,0:T(8,128)S(1)}, u32[]{:S(2)}, u32[]{:S(2)}) collective-permute-start(f32[128,128]{1,0:T(8,128)S(1)} %get-tuple-element.51.one_ref), channel_id=1, source_target_pairs={{0,2},{1,3},{2,0},{3,1},{4,6},{5,7},{6,4},{7,5},{8,10},{9,11},{10,... | collective-permute-start | bytes 196616 | tf_op jit(solution)/shard_map/ppermute | solution.py:358
  32.2 4.3 %collective-permute-start.3 = (f32[128,128]{1,0:T(8,128)S(1)}, f32[128,128]{1,0:T(8,128)S(1)}, u32[]{:S(2)}, u32[]{:S(2)}) collective-permute-start(f32[128,128]{1,0:T(8,128)S(1)} %add.16.one_ref), channel_id=1, source_target_pairs={{0,2},{1,3},{2,0},{3,1},{4,6},{5,7},{6,4},{7,5},{8,10},{9,11},{10,... | collective-permute-start | bytes 196616 | tf_op jit(solution)/shard_map/ppermute | solution.py:358
  34.1 5.3 %collective-permute-start.6 = (f32[128,128]{1,0:T(8,128)S(1)}, f32[128,128]{1,0:T(8,128)S(1)}, u32[]{:S(2)}, u32[]{:S(2)}) collective-permute-start(f32[128,128]{1,0:T(8,128)S(1)} %add.18.one_ref), channel_id=1, source_target_pairs={{0,1},{1,0},{2,3},{3,2},{4,5},{5,4},{6,7},{7,6},{8,9},{9,8},{10,11... | collective-permute-start | bytes 196616 | tf_op jit(solution)/shard_map/ppermute | solution.py:358
  36.6 7.3 %collective-permute-start.4 = (f32[128,128]{1,0:T(8,128)S(1)}, f32[128,128]{1,0:T(8,128)S(1)}, u32[]{:S(2)}, u32[]{:S(2)}) collective-permute-start(f32[128,128]{1,0:T(8,128)S(1)} %add.17.front), channel_id=1, source_target_pairs={{0,4},{1,5},{2,6},{3,7},{4,0},{5,1},{6,2},{7,3},{8,12},{9,13},{10,... | collective-permute-start | bytes 196616 | tf_op jit(solution)/shard_map/ppermute | solution.py:358
  39.5 5.2 %collective-permute-start.7 = (f32[128,128]{1,0:T(8,128)S(1)}, f32[128,128]{1,0:T(8,128)S(1)}, u32[]{:S(2)}, u32[]{:S(2)}) collective-permute-start(f32[128,128]{1,0:T(8,128)S(1)} %add.19.back), channel_id=1, source_target_pairs={{0,4},{1,5},{2,6},{3,7},{4,0},{5,1},{6,2},{7,3},{8,12},{9,13},{10,... | collective-permute-start | bytes 196616 | tf_op jit(solution)/shard_map/ppermute | solution.py:358
  44.7 2.2 %collective-permute-start.8 = (f32[32,1024]{1,0:T(8,128)S(1)}, f32[32,1024]{1,0:T(8,128)S(1)}, u32[]{:S(2)}, u32[]{:S(2)}) collective-permute-start(f32[32,1024]{1,0:T(8,128)S(1)} %get-tuple-element.52.clipped_ref), channel_id=1, source_target_pairs={{0,8},{8,0},{1,9},{9,1},{2,10},{10,2},{3,11},{11,3},{4,12},{12,4},... | collective-permute-start | bytes 393224 | tf_op jit(solution)/shard_map/ppermute | solution.py:348
  52.6 4.0 %collective-permute-start.9 = (f32[264,128]{1,0:T(8,128)S(1)}, f32[264,128]{1,0:T(8,128)S(1)}, u32[]{:S(2)}, u32[]{:S(2)}) collective-permute-start(f32[264,128]{1,0:T(8,128)S(1)} %get-tuple-element.59), channel_id=1, source_target_pairs={{0,8},{8,0},{1,9},{9,1},{2,10},{10,2},{3,11},{11,3},{4,12},{12,4},... | collective-permute-start | bytes 405512 | tf_op jit(solution)/shard_map/ppermute | solution.py:348
  56.6 4.4 %collective-permute-start.10 = (f32[136,128]{1,0:T(8,128)S(1)}, f32[136,128]{1,0:T(8,128)S(1)}, u32[]{:S(2)}, u32[]{:S(2)}) collective-permute-start(f32[136,128]{1,0:T(8,128)S(1)} %get-tuple-element.60.one_ref), channel_id=1, source_target_pairs={{0,1},{1,0},{2,3},{3,2},{4,5},{5,4},{6,7},{7,6},{8,9},{9,8},{10,11... | collective-permute-start | bytes 208904 | tf_op jit(solution)/shard_map/ppermute | solution.py:358
  58.2 4.4 %collective-permute-start.13 = (f32[128,128]{1,0:T(8,128)S(1)}, f32[128,128]{1,0:T(8,128)S(1)}, u32[]{:S(2)}, u32[]{:S(2)}) collective-permute-start(f32[128,128]{1,0:T(8,128)S(1)} %get-tuple-element.61.one_ref), channel_id=1, source_target_pairs={{0,2},{1,3},{2,0},{3,1},{4,6},{5,7},{6,4},{7,5},{8,10},{9,11},{10,... | collective-permute-start | bytes 196616 | tf_op jit(solution)/shard_map/ppermute | solution.py:358
  61.0 4.4 %collective-permute-start.11 = (f32[136,128]{1,0:T(8,128)S(1)}, f32[136,128]{1,0:T(8,128)S(1)}, u32[]{:S(2)}, u32[]{:S(2)}) collective-permute-start(f32[136,128]{1,0:T(8,128)S(1)} %add.20.one_ref), channel_id=1, source_target_pairs={{0,2},{1,3},{2,0},{3,1},{4,6},{5,7},{6,4},{7,5},{8,10},{9,11},{10,... | collective-permute-start | bytes 208904 | tf_op jit(solution)/shard_map/ppermute | solution.py:358
  62.7 4.5 %collective-permute-start.14 = (f32[128,128]{1,0:T(8,128)S(1)}, f32[128,128]{1,0:T(8,128)S(1)}, u32[]{:S(2)}, u32[]{:S(2)}) collective-permute-start(f32[128,128]{1,0:T(8,128)S(1)} %add.22.one_ref), channel_id=1, source_target_pairs={{0,1},{1,0},{2,3},{3,2},{4,5},{5,4},{6,7},{7,6},{8,9},{9,8},{10,11... | collective-permute-start | bytes 196616 | tf_op jit(solution)/shard_map/ppermute | solution.py:358
  65.4 7.1 %collective-permute-start.12 = (f32[136,128]{1,0:T(8,128)S(1)}, f32[136,128]{1,0:T(8,128)S(1)}, u32[]{:S(2)}, u32[]{:S(2)}) collective-permute-start(f32[136,128]{1,0:T(8,128)S(1)} %add.21.front), channel_id=1, source_target_pairs={{0,4},{1,5},{2,6},{3,7},{4,0},{5,1},{6,2},{7,3},{8,12},{9,13},{10,... | collective-permute-start | bytes 208904 | tf_op jit(solution)/shard_map/ppermute | solution.py:358
  67.2 5.3 %collective-permute-start.15 = (f32[128,128]{1,0:T(8,128)S(1)}, f32[128,128]{1,0:T(8,128)S(1)}, u32[]{:S(2)}, u32[]{:S(2)}) collective-permute-start(f32[128,128]{1,0:T(8,128)S(1)} %add.23.back), channel_id=1, source_target_pairs={{0,4},{1,5},{2,6},{3,7},{4,0},{5,1},{6,2},{7,3},{8,12},{9,13},{10,... | collective-permute-start | bytes 196616 | tf_op jit(solution)/shard_map/ppermute | solution.py:358
  80.7 4.0 %collective-permute-start.17 = (f32[264,128]{1,0:T(8,128)S(1)}, f32[264,128]{1,0:T(8,128)S(1)}, u32[]{:S(2)}, u32[]{:S(2)}) collective-permute-start(f32[264,128]{1,0:T(8,128)S(1)} %get-tuple-element.67), channel_id=1, source_target_pairs={{0,8},{8,0},{1,9},{9,1},{2,10},{10,2},{3,11},{11,3},{4,12},{12,4},... | collective-permute-start | bytes 405512 | tf_op jit(solution)/shard_map/ppermute | solution.py:348
  84.8 4.4 %collective-permute-start.18 = (f32[136,128]{1,0:T(8,128)S(1)}, f32[136,128]{1,0:T(8,128)S(1)}, u32[]{:S(2)}, u32[]{:S(2)}) collective-permute-start(f32[136,128]{1,0:T(8,128)S(1)} %get-tuple-element.68.one_ref), channel_id=1, source_target_pairs={{0,1},{1,0},{2,3},{3,2},{4,5},{5,4},{6,7},{7,6},{8,9},{9,8},{10,11... | collective-permute-start | bytes 208904 | tf_op jit(solution)/shard_map/ppermute | solution.py:358
  86.4 4.8 %collective-permute-start.21 = (f32[128,128]{1,0:T(8,128)S(1)}, f32[128,128]{1,0:T(8,128)S(1)}, u32[]{:S(2)}, u32[]{:S(2)}) collective-permute-start(f32[128,128]{1,0:T(8,128)S(1)} %get-tuple-element.69.one_ref), channel_id=1, source_target_pairs={{0,2},{1,3},{2,0},{3,1},{4,6},{5,7},{6,4},{7,5},{8,10},{9,11},{10,... | collective-permute-start | bytes 196616 | tf_op jit(solution)/shard_map/ppermute | solution.py:358
  89.2 4.4 %collective-permute-start.19 = (f32[136,128]{1,0:T(8,128)S(1)}, f32[136,128]{1,0:T(8,128)S(1)}, u32[]{:S(2)}, u32[]{:S(2)}) collective-permute-start(f32[136,128]{1,0:T(8,128)S(1)} %add.24.one_ref), channel_id=1, source_target_pairs={{0,2},{1,3},{2,0},{3,1},{4,6},{5,7},{6,4},{7,5},{8,10},{9,11},{10,... | collective-permute-start | bytes 208904 | tf_op jit(solution)/shard_map/ppermute | solution.py:358
  91.1 4.4 %collective-permute-start.22 = (f32[128,128]{1,0:T(8,128)S(1)}, f32[128,128]{1,0:T(8,128)S(1)}, u32[]{:S(2)}, u32[]{:S(2)}) collective-permute-start(f32[128,128]{1,0:T(8,128)S(1)} %add.26.one_ref), channel_id=1, source_target_pairs={{0,1},{1,0},{2,3},{3,2},{4,5},{5,4},{6,7},{7,6},{8,9},{9,8},{10,11... | collective-permute-start | bytes 196616 | tf_op jit(solution)/shard_map/ppermute | solution.py:358
  93.5 7.4 %collective-permute-start.20 = (f32[136,128]{1,0:T(8,128)S(1)}, f32[136,128]{1,0:T(8,128)S(1)}, u32[]{:S(2)}, u32[]{:S(2)}) collective-permute-start(f32[136,128]{1,0:T(8,128)S(1)} %add.25.front), channel_id=1, source_target_pairs={{0,4},{1,5},{2,6},{3,7},{4,0},{5,1},{6,2},{7,3},{8,12},{9,13},{10,... | collective-permute-start | bytes 208904 | tf_op jit(solution)/shard_map/ppermute | solution.py:358
  95.6 5.3 %collective-permute-start.23 = (f32[128,128]{1,0:T(8,128)S(1)}, f32[128,128]{1,0:T(8,128)S(1)}, u32[]{:S(2)}, u32[]{:S(2)}) collective-permute-start(f32[128,128]{1,0:T(8,128)S(1)} %add.27.back), channel_id=1, source_target_pairs={{0,4},{1,5},{2,6},{3,7},{4,0},{5,1},{6,2},{7,3},{8,12},{9,13},{10,... | collective-permute-start | bytes 196616 | tf_op jit(solution)/shard_map/ppermute | solution.py:358
  101.1 2.9 %collective-permute-start.24 = (f32[32,1024]{1,0:T(8,128)S(1)}, f32[32,1024]{1,0:T(8,128)S(1)}, u32[]{:S(2)}, u32[]{:S(2)}) collective-permute-start(f32[32,1024]{1,0:T(8,128)S(1)} %get-tuple-element.72.clipped_ref), channel_id=1, source_target_pairs={{0,8},{8,0},{1,9},{9,1},{2,10},{10,2},{3,11},{11,3},{4,12},{12,4},... | collective-permute-start | bytes 393224 | tf_op jit(solution)/shard_map/ppermute | solution.py:348
  103.4 26.4 %collective-permute-start.32 = (f32[32,4096]{1,0:T(8,128)S(1)}, f32[32,4096]{1,0:T(8,128)S(1)}, u32[]{:S(2)}, u32[]{:S(2)}) collective-permute-start(f32[32,4096]{1,0:T(8,128)S(1)} %sum.1.refs_1_), channel_id=1, source_target_pairs={{0,8},{8,0},{1,9},{9,1},{2,10},{10,2},{3,11},{11,3},{4,12},{12,4},... | collective-permute-start | bytes 1572872 | tf_op jit(solution)/shard_map/ppermute | solution.py:348
  109.6 20.1 %collective-permute-start.33 = (f32[32,4096]{1,0:T(8,128)S(1)}, f32[32,4096]{1,0:T(8,128)S(1)}, u32[]{:S(2)}, u32[]{:S(2)}) collective-permute-start(f32[32,4096]{1,0:T(8,128)S(1)} %get-tuple-element.85.refs_3_), channel_id=1, source_target_pairs={{0,8},{8,0},{1,9},{9,1},{2,10},{10,2},{3,11},{11,3},{4,12},{12,4},... | collective-permute-start | bytes 1572872 | tf_op jit(solution)/shard_map/ppermute | solution.py:348
  109.7 3.9 %collective-permute-start.25 = (f32[264,128]{1,0:T(8,128)S(1)}, f32[264,128]{1,0:T(8,128)S(1)}, u32[]{:S(2)}, u32[]{:S(2)}) collective-permute-start(f32[264,128]{1,0:T(8,128)S(1)} %get-tuple-element.76), channel_id=1, source_target_pairs={{0,8},{8,0},{1,9},{9,1},{2,10},{10,2},{3,11},{11,3},{4,12},{12,4},... | collective-permute-start | bytes 405512 | tf_op jit(solution)/shard_map/ppermute | solution.py:348
  113.7 4.4 %collective-permute-start.26 = (f32[136,128]{1,0:T(8,128)S(1)}, f32[136,128]{1,0:T(8,128)S(1)}, u32[]{:S(2)}, u32[]{:S(2)}) collective-permute-start(f32[136,128]{1,0:T(8,128)S(1)} %get-tuple-element.77.one_ref), channel_id=1, source_target_pairs={{0,1},{1,0},{2,3},{3,2},{4,5},{5,4},{6,7},{7,6},{8,9},{9,8},{10,11... | collective-permute-start | bytes 208904 | tf_op jit(solution)/shard_map/ppermute | solution.py:358
  115.2 4.8 %collective-permute-start.29 = (f32[128,128]{1,0:T(8,128)S(1)}, f32[128,128]{1,0:T(8,128)S(1)}, u32[]{:S(2)}, u32[]{:S(2)}) collective-permute-start(f32[128,128]{1,0:T(8,128)S(1)} %get-tuple-element.78.one_ref), channel_id=1, source_target_pairs={{0,2},{1,3},{2,0},{3,1},{4,6},{5,7},{6,4},{7,5},{8,10},{9,11},{10,... | collective-permute-start | bytes 196616 | tf_op jit(solution)/shard_map/ppermute | solution.py:358
  118.1 4.4 %collective-permute-start.27 = (f32[136,128]{1,0:T(8,128)S(1)}, f32[136,128]{1,0:T(8,128)S(1)}, u32[]{:S(2)}, u32[]{:S(2)}) collective-permute-start(f32[136,128]{1,0:T(8,128)S(1)} %add.28.one_ref), channel_id=1, source_target_pairs={{0,2},{1,3},{2,0},{3,1},{4,6},{5,7},{6,4},{7,5},{8,10},{9,11},{10,... | collective-permute-start | bytes 208904 | tf_op jit(solution)/shard_map/ppermute | solution.py:358
  120.1 4.4 %collective-permute-start.30 = (f32[128,128]{1,0:T(8,128)S(1)}, f32[128,128]{1,0:T(8,128)S(1)}, u32[]{:S(2)}, u32[]{:S(2)}) collective-permute-start(f32[128,128]{1,0:T(8,128)S(1)} %add.30.one_ref), channel_id=1, source_target_pairs={{0,1},{1,0},{2,3},{3,2},{4,5},{5,4},{6,7},{7,6},{8,9},{9,8},{10,11... | collective-permute-start | bytes 196616 | tf_op jit(solution)/shard_map/ppermute | solution.py:358
  122.5 7.3 %collective-permute-start.28 = (f32[136,128]{1,0:T(8,128)S(1)}, f32[136,128]{1,0:T(8,128)S(1)}, u32[]{:S(2)}, u32[]{:S(2)}) collective-permute-start(f32[136,128]{1,0:T(8,128)S(1)} %add.29.front), channel_id=1, source_target_pairs={{0,4},{1,5},{2,6},{3,7},{4,0},{5,1},{6,2},{7,3},{8,12},{9,13},{10,... | collective-permute-start | bytes 208904 | tf_op jit(solution)/shard_map/ppermute | solution.py:358
  124.5 5.3 %collective-permute-start.31 = (f32[128,128]{1,0:T(8,128)S(1)}, f32[128,128]{1,0:T(8,128)S(1)}, u32[]{:S(2)}, u32[]{:S(2)}) collective-permute-start(f32[128,128]{1,0:T(8,128)S(1)} %add.31.back), channel_id=1, source_target_pairs={{0,4},{1,5},{2,6},{3,7},{4,0},{5,1},{6,2},{7,3},{8,12},{9,13},{10,... | collective-permute-start | bytes 196616 | tf_op jit(solution)/shard_map/ppermute | solution.py:358
  (4 other events, 64.5 us)

commit v3 on v2

--- a/solution.py
+++ b/solution.py
@@ -271,8 +271,8 @@
         clipped_out[:, span] = jnp.clip(predicted - targets_ref[:, span], -huber_cap, huber_cap)
 
 
-def inverse_of(entries, front, front_last, back):
-    end = pl.ds(back.shape[0], 8)
+def inverse_of(entries, front, front_last, start):
+    end = pl.ds(start, 8)
     total = jnp.sum(front[end, :] + front_last[end, :], axis=(0, 1), keepdims=True)
     return 1.0 / jnp.sqrt(total / entries + epsilon)
 
@@ -280,7 +280,7 @@
 def step_kernel(entries, front, front_last, back, back_last, targets_ref, predicted_ref, *refs):
     tracked_ref = refs[0] if len(refs) == 5 else None
     clipped_out, predicted_out, inverse_out, tracked_out = refs[-4:]
-    inverse = inverse_of(entries, front, front_last, back)
+    inverse = inverse_of(entries, front, front_last, back.shape[0])
     inverse_out[...] = jnp.broadcast_to(inverse, (8, 128))
     for span, (one, other), rows in places(targets_ref, (front, front_last), (back, back_last)):
         tracked = (one[rows, :] + other[rows, :]) * inverse
@@ -299,18 +299,23 @@
     refs[-1][...] = total
 
 
-def close_kernel(entries, weight, front, front_last, back, back_last, targets_ref, predicted_ref, tracked_ref, *refs):
-    coeffs_ref, taken_ref, other_taken, grad_ref, other_grad, predicted_out, coeffs_out = refs
-    inverse = inverse_of(entries, front, front_last, back)
-    for span, (one, other), rows in places(targets_ref, (front, front_last), (back, back_last)):
-        tracked = momentum * tracked_ref[:, span] + (one[rows, :] + other[rows, :]) * inverse
-        predicted_out[:, span] = predicted_ref[:, span] - step_rate * tracked
+def close_kernel(entries, weight, front, front_last, *refs):
+    coeffs_ref, taken_ref, other_taken, grad_ref, other_grad, coeffs_out, inverse_out = refs
+    inverse = inverse_of(entries, front, front_last, front.shape[0] - 8)
+    inverse_out[...] = jnp.broadcast_to(inverse, (8, 128))
     width = taken_ref.shape[1]
     core = lax.axis_index("paths")
     factor = weight * inverse
     for start, taken, grad in ((core, taken_ref, grad_ref), (1 - core, other_taken, other_grad)):
         span = pl.ds(pl.multiple_of(start * width, width), width)
         coeffs_out[:, span] = coeffs_ref[:, span] - (taken[...] + factor * grad[...])
+
+
+def last_kernel(front, front_last, back, back_last, predicted_ref, tracked_ref, inverse_ref, predicted_out):
+    inverse = inverse_ref[0:1, 0:1]
+    for span, (one, other), rows in places(predicted_ref, (front, front_last), (back, back_last)):
+        tracked = momentum * tracked_ref[:, span] + (one[rows, :] + other[rows, :]) * inverse
+        predicted_out[:, span] = predicted_ref[:, span] - step_rate * tracked
 
 
 def vmem(count):
@@ -435,6 +440,7 @@
         halves = call(join_kernel, "join", (image_own, swap(image_other)), ((middle + 8, 128), (middle, 128)))
         grads.append(grad)
         if turn == ITERS - 1:
+            sums = all_chips(*halves)
             break
         clipped, predicted, inverse, *tracked = call(
             functools.partial(step_kernel, entries),
@@ -445,15 +451,16 @@
         inverses.append(inverse)
     before = [array for pair in zip(grads, inverses) for array in pair]
     taken = call(functools.partial(sum_kernel, weights[:-1]), "sum", before, (wide,))[0]
-    predicted, coeffs = call(
+    coeffs, inverse = call(
         functools.partial(close_kernel, entries, weights[-1]),
         "close",
-        (*all_chips(*halves), targets, predicted, *tracked, coeffs_init, taken, swap(taken), grad, swap(grad)),
-        (small, (count, width * cores)),
+        (*sums[:2], coeffs_init, taken, swap(taken), grad, swap(grad)),
+        ((count, width * cores), (8, 128)),
         None,
         (),
         8,
     )
+    predicted = call(last_kernel, "last", (*sums, predicted, *tracked, inverse), (small,))[0]
     return (coeffs, predicted)
 
 

time: 131 us -> 131 us (level)
  waiting for transfers between devices: 23.9 us -> 22.5 us
    ppermute x24, waiting for transfers between devices: 22.6 us -> 21.1 us  [all_chips(): lax.ppermute(array, 'feats', [(chip, chip ^ order[step]) for chip in rang...]
    pallas_call x36 -> x37, Pallas kernels: 60.1 us -> 60.9 us  [call(): pl.pallas_call(kernel, out_shape=shapes, in_specs=specs or vmem(len(argum...]
  transfers between devices with their start and end apart: 34 -> 34, of which waited for: 14 -> 15; matrix products, arithmetic and copies ran while one was open for 0% -> 0% of each run, Pallas kernels for 19% -> 20%
where the time goes in v3:
time: 131 us
  Pallas kernels  60.9 us (46%)
  starting transfers between devices  46.3 us (35%)
  waiting for transfers between devices  22.5 us (17%)
    pallas_call x37, Pallas kernels, call(): pl.pallas_call(kernel, out_shape=shapes, in_specs=specs or vmem(len(argum...  60.9 us
    ppermute x24, starting transfers between devices, all_chips(): lax.ppermute(array, 'feats', [(chip, chip ^ order[step]) for chip in rang...  43.2 us
    ppermute x24, waiting for transfers between devices, all_chips(): lax.ppermute(array, 'feats', [(chip, chip ^ order[step]) for chip in rang...  21.1 us
    ppermute x10, starting transfers between devices, swap(): return lax.ppermute(array, 'paths', [(0, 1), (1, 0)])  3.13 us
  transfers between devices with their start and end apart: 34, of which 15 were waited for; matrix products, arithmetic and copies ran while one was open for 0% of the time, Pallas kernels for 20%

profile of v3, /device:TPU:0, one launch (start us, length us, event | category | flops | bytes accessed | tf_op | source)
XLA Modules:
  0.0 130.5 jit_solution(3204554212497378094)
XLA Ops:
  1.1 2.1 %prepare.1 = (bf16[1024,256]{1,0:T(8,128)(2,1)S(1)}, bf16[256,4096]{1,0:T(8,128)(2,1)S(1)}, bf16[64,4096]{1,0:T(8,128)(2,1)S(1)}, f32[1,4096]{1,0:T(1,128)S(1)}) custom-call(s32[1024,128]{1,0:T(8,128)} %own_ref.1, s32[128,8192]{1,0:T(8,128)} %freq_ref.1, s32[1,8192]{1,0:T(1,128)} %bitcast.2, f32[1,8192]{1,0:T(1,128)} %bitcast.3, f32[32,8192]{1,0:T(8,128)} %refs_0_.1), custom_call_target="tpu_custom_call" | custom-call | tf_op jit(solution)/shard_map/prepare/pallas_call | solution.py:331
  3.3 22.1 %build.1 = (f32[32,1024]{1,0:T(8,128)S(1)}, f32[32,1024]{1,0:T(8,128)S(1)}, bf16[2048,4096]{1,0:T(8,128)(2,1)S(1)}, f8e4m3fn[2048,4096]{1,0:T(32,128)(4,1)S(1)}) custom-call(bf16[1024,256]{1,0:T(8,128)(2,1)S(1)} %get-tuple-element.45.own_ref, s32[1024,128]{1,0:T(8,128)S(1)} %collective-permute-done.other_ref, ...), custom_call_target="tpu_custom_call", output_to_operand_aliasing={{2}: (4, {}), {3}: (5, {})} | custom-call | tf_op jit(solution)/shard_map/build/pallas_call | solution.py:331
  26.9 2.7 %collective-permute-start.2 = (f32[128,128]{1,0:T(8,128)S(1)}, f32[128,128]{1,0:T(8,128)S(1)}, u32[]{:S(2)}, u32[]{:S(2)}) collective-permute-start(f32[128,128]{1,0:T(8,128)S(1)} %get-tuple-element.50.one_ref), channel_id=1, source_target_pairs={{0,1},{1,0},{2,3},{3,2},{4,5},{5,4},{6,7},{7,6},{8,9},{9,8},{10,11... | collective-permute-start | bytes 196616 | tf_op jit(solution)/shard_map/ppermute | solution.py:363
  32.3 1.9 %collective-permute-start.3 = (f32[128,128]{1,0:T(8,128)S(1)}, f32[128,128]{1,0:T(8,128)S(1)}, u32[]{:S(2)}, u32[]{:S(2)}) collective-permute-start(f32[128,128]{1,0:T(8,128)S(1)} %add.16.one_ref), channel_id=1, source_target_pairs={{0,2},{1,3},{2,0},{3,1},{4,6},{5,7},{6,4},{7,5},{8,10},{9,11},{10,... | collective-permute-start | bytes 196616 | tf_op jit(solution)/shard_map/ppermute | solution.py:363
  34.1 1.6 %collective-permute-start.6 = (f32[128,128]{1,0:T(8,128)S(1)}, f32[128,128]{1,0:T(8,128)S(1)}, u32[]{:S(2)}, u32[]{:S(2)}) collective-permute-start(f32[128,128]{1,0:T(8,128)S(1)} %add.18.one_ref), channel_id=1, source_target_pairs={{0,1},{1,0},{2,3},{3,2},{4,5},{5,4},{6,7},{7,6},{8,9},{9,8},{10,11... | collective-permute-start | bytes 196616 | tf_op jit(solution)/shard_map/ppermute | solution.py:363
  36.6 2.9 %collective-permute-start.4 = (f32[128,128]{1,0:T(8,128)S(1)}, f32[128,128]{1,0:T(8,128)S(1)}, u32[]{:S(2)}, u32[]{:S(2)}) collective-permute-start(f32[128,128]{1,0:T(8,128)S(1)} %add.17.front), channel_id=1, source_target_pairs={{0,4},{1,5},{2,6},{3,7},{4,0},{5,1},{6,2},{7,3},{8,12},{9,13},{10,... | collective-permute-start | bytes 196616 | tf_op jit(solution)/shard_map/ppermute | solution.py:363
  39.5 1.6 %collective-permute-start.7 = (f32[128,128]{1,0:T(8,128)S(1)}, f32[128,128]{1,0:T(8,128)S(1)}, u32[]{:S(2)}, u32[]{:S(2)}) collective-permute-start(f32[128,128]{1,0:T(8,128)S(1)} %add.19.back), channel_id=1, source_target_pairs={{0,4},{1,5},{2,6},{3,7},{4,0},{5,1},{6,2},{7,3},{8,12},{9,13},{10,... | collective-permute-start | bytes 196616 | tf_op jit(solution)/shard_map/ppermute | solution.py:363
  41.1 2.8 %collective-permute-done.4.front_last = f32[128,128]{1,0:T(8,128)S(1)} collective-permute-done((f32[128,128]{1,0:T(8,128)S(1)}, f32[128,128]{1,0:T(8,128)S(1)}, u32[]{:S(2)}, u32[]{:S(2)}) %collective-permute-start.4) | collective-permute-done | bytes 65568 | tf_op jit(solution)/shard_map/ppermute | solution.py:363
  44.8 2.1 %own.3.partial_ref = f32[32,4096]{1,0:T(8,128)S(1)} custom-call(f32[32,1024]{1,0:T(8,128)S(1)} %get-tuple-element.52.clipped_ref, bf16[2048,4096]{1,0:T(8,128)(2,1)S(1)} %get-tuple-element.53.high_ref, f8e4m3fn[2048,4096]{1,0:T(32,128)(4,1)S(1)} %get-tuple-element.54.low_ref), custom_call_target="tpu_custom_call" | custom-call | tf_op jit(solution)/shard_map/own/pallas_call | solution.py:331
  47.0 5.7 %rest.3 = (f32[32,4096]{1,0:T(8,128)S(1)}, bf16[64,4096]{1,0:T(8,128)(2,1)S(1)}, f8e4m3fn[32,4096]{1,0:T(32,128)(4,1)S(1)}, f32[264,128]{1,0:T(8,128)S(1)}, f32[40,128]{1,0:T(8,128)S(1)}) custom-call(f32[32,1024]{1,0:T(8,128)S(1)} %collective-permute-done.8.clipped_ref, bf16[2048,4096]{1,0:T(8,128)(2,1)S(1)} %get-tuple-element.53.high_ref, ...), custom_call_target="tpu_custom_call" | custom-call | tf_op jit(solution)/shard_map/rest/pallas_call | solution.py:331
  53.2 3.4 %image.3.own_ref = f32[264,128]{1,0:T(8,128)S(1)} custom-call(bf16[64,4096]{1,0:T(8,128)(2,1)S(1)} %get-tuple-element.56.pair_ref, f8e4m3fn[32,4096]{1,0:T(32,128)(4,1)S(1)} %get-tuple-element.57.coarse_ref, f32[40,128]{1,0:T(8,128)S(1)} %get-tuple-element.58.notes_ref, bf16[2048,4096]{1,0:T(8,128)(2,1)S(1)} %get-tuple-element.53.high_ref, ...), custom_call_target="tpu_custom_call" | custom-call | tf_op jit(solution)/shard_map/image/pallas_call | solution.py:331
  56.7 1.6 %collective-permute-start.10 = (f32[136,128]{1,0:T(8,128)S(1)}, f32[136,128]{1,0:T(8,128)S(1)}, u32[]{:S(2)}, u32[]{:S(2)}) collective-permute-start(f32[136,128]{1,0:T(8,128)S(1)} %get-tuple-element.60.one_ref), channel_id=1, source_target_pairs={{0,1},{1,0},{2,3},{3,2},{4,5},{5,4},{6,7},{7,6},{8,9},{9,8},{10,11... | collective-permute-start | bytes 208904 | tf_op jit(solution)/shard_map/ppermute | solution.py:363
  61.0 1.6 %collective-permute-start.11 = (f32[136,128]{1,0:T(8,128)S(1)}, f32[136,128]{1,0:T(8,128)S(1)}, u32[]{:S(2)}, u32[]{:S(2)}) collective-permute-start(f32[136,128]{1,0:T(8,128)S(1)} %add.20.one_ref), channel_id=1, source_target_pairs={{0,2},{1,3},{2,0},{3,1},{4,6},{5,7},{6,4},{7,5},{8,10},{9,11},{10,... | collective-permute-start | bytes 208904 | tf_op jit(solution)/shard_map/ppermute | solution.py:363
  62.7 1.6 %collective-permute-start.14 = (f32[128,128]{1,0:T(8,128)S(1)}, f32[128,128]{1,0:T(8,128)S(1)}, u32[]{:S(2)}, u32[]{:S(2)}) collective-permute-start(f32[128,128]{1,0:T(8,128)S(1)} %add.22.one_ref), channel_id=1, source_target_pairs={{0,1},{1,0},{2,3},{3,2},{4,5},{5,4},{6,7},{7,6},{8,9},{9,8},{10,11... | collective-permute-start | bytes 196616 | tf_op jit(solution)/shard_map/ppermute | solution.py:363
  65.4 1.8 %collective-permute-start.12 = (f32[136,128]{1,0:T(8,128)S(1)}, f32[136,128]{1,0:T(8,128)S(1)}, u32[]{:S(2)}, u32[]{:S(2)}) collective-permute-start(f32[136,128]{1,0:T(8,128)S(1)} %add.21.front), channel_id=1, source_target_pairs={{0,4},{1,5},{2,6},{3,7},{4,0},{5,1},{6,2},{7,3},{8,12},{9,13},{10,... | collective-permute-start | bytes 208904 | tf_op jit(solution)/shard_map/ppermute | solution.py:363
  67.2 2.0 %collective-permute-start.15 = (f32[128,128]{1,0:T(8,128)S(1)}, f32[128,128]{1,0:T(8,128)S(1)}, u32[]{:S(2)}, u32[]{:S(2)}) collective-permute-start(f32[128,128]{1,0:T(8,128)S(1)} %add.23.back), channel_id=1, source_target_pairs={{0,4},{1,5},{2,6},{3,7},{4,0},{5,1},{6,2},{7,3},{8,12},{9,13},{10,... | collective-permute-start | bytes 196616 | tf_op jit(solution)/shard_map/ppermute | solution.py:363
  69.3 3.3 %collective-permute-done.15.back_last = f32[128,128]{1,0:T(8,128)S(1)} collective-permute-done((f32[128,128]{1,0:T(8,128)S(1)}, f32[128,128]{1,0:T(8,128)S(1)}, u32[]{:S(2)}, u32[]{:S(2)}) %collective-permute-start.15) | collective-permute-done | bytes 65568 | tf_op jit(solution)/shard_map/ppermute | solution.py:363
  72.8 2.1 %own.4.partial_ref = f32[32,4096]{1,0:T(8,128)S(1)} custom-call(f32[32,1024]{1,0:T(8,128)S(1)} %get-tuple-element.63.clipped_ref, bf16[2048,4096]{1,0:T(8,128)(2,1)S(1)} %get-tuple-element.53.high_ref, f8e4m3fn[2048,4096]{1,0:T(32,128)(4,1)S(1)} %get-tuple-element.54.low_ref), custom_call_target="tpu_custom_call" | custom-call | tf_op jit(solution)/shard_map/own/pallas_call | solution.py:331
  74.9 5.9 %rest.4 = (f32[32,4096]{1,0:T(8,128)S(1)}, bf16[64,4096]{1,0:T(8,128)(2,1)S(1)}, f8e4m3fn[32,4096]{1,0:T(32,128)(4,1)S(1)}, f32[264,128]{1,0:T(8,128)S(1)}, f32[40,128]{1,0:T(8,128)S(1)}) custom-call(f32[32,1024]{1,0:T(8,128)S(1)} %collective-permute-done.16.clipped_ref, bf16[2048,4096]{1,0:T(8,128)(2,1)S(1)} %get-tuple-element.53.high_ref, ...), custom_call_target="tpu_custom_call" | custom-call | tf_op jit(solution)/shard_map/rest/pallas_call | solution.py:331
  81.3 3.4 %image.4.own_ref = f32[264,128]{1,0:T(8,128)S(1)} custom-call(bf16[64,4096]{1,0:T(8,128)(2,1)S(1)} %get-tuple-element.64.pair_ref, f8e4m3fn[32,4096]{1,0:T(32,128)(4,1)S(1)} %get-tuple-element.65.coarse_ref, f32[40,128]{1,0:T(8,128)S(1)} %get-tuple-element.66.notes_ref, bf16[2048,4096]{1,0:T(8,128)(2,1)S(1)} %get-tuple-element.53.high_ref, ...), custom_call_target="tpu_custom_call" | custom-call | tf_op jit(solution)/shard_map/image/pallas_call | solution.py:331
  84.8 1.6 %collective-permute-start.18 = (f32[136,128]{1,0:T(8,128)S(1)}, f32[136,128]{1,0:T(8,128)S(1)}, u32[]{:S(2)}, u32[]{:S(2)}) collective-permute-start(f32[136,128]{1,0:T(8,128)S(1)} %get-tuple-element.68.one_ref), channel_id=1, source_target_pairs={{0,1},{1,0},{2,3},{3,2},{4,5},{5,4},{6,7},{7,6},{8,9},{9,8},{10,11... | collective-permute-start | bytes 208904 | tf_op jit(solution)/shard_map/ppermute | solution.py:363
  86.4 1.9 %collective-permute-start.21 = (f32[128,128]{1,0:T(8,128)S(1)}, f32[128,128]{1,0:T(8,128)S(1)}, u32[]{:S(2)}, u32[]{:S(2)}) collective-permute-start(f32[128,128]{1,0:T(8,128)S(1)} %get-tuple-element.69.one_ref), channel_id=1, source_target_pairs={{0,2},{1,3},{2,0},{3,1},{4,6},{5,7},{6,4},{7,5},{8,10},{9,11},{10,... | collective-permute-start | bytes 196616 | tf_op jit(solution)/shard_map/ppermute | solution.py:363
  89.2 2.0 %collective-permute-start.19 = (f32[136,128]{1,0:T(8,128)S(1)}, f32[136,128]{1,0:T(8,128)S(1)}, u32[]{:S(2)}, u32[]{:S(2)}) collective-permute-start(f32[136,128]{1,0:T(8,128)S(1)} %add.24.one_ref), channel_id=1, source_target_pairs={{0,2},{1,3},{2,0},{3,1},{4,6},{5,7},{6,4},{7,5},{8,10},{9,11},{10,... | collective-permute-start | bytes 208904 | tf_op jit(solution)/shard_map/ppermute | solution.py:363
  93.6 2.0 %collective-permute-start.20 = (f32[136,128]{1,0:T(8,128)S(1)}, f32[136,128]{1,0:T(8,128)S(1)}, u32[]{:S(2)}, u32[]{:S(2)}) collective-permute-start(f32[136,128]{1,0:T(8,128)S(1)} %add.25.front), channel_id=1, source_target_pairs={{0,4},{1,5},{2,6},{3,7},{4,0},{5,1},{6,2},{7,3},{8,12},{9,13},{10,... | collective-permute-start | bytes 208904 | tf_op jit(solution)/shard_map/ppermute | solution.py:363
  95.6 2.0 %collective-permute-start.23 = (f32[128,128]{1,0:T(8,128)S(1)}, f32[128,128]{1,0:T(8,128)S(1)}, u32[]{:S(2)}, u32[]{:S(2)}) collective-permute-start(f32[128,128]{1,0:T(8,128)S(1)} %add.27.back), channel_id=1, source_target_pairs={{0,4},{1,5},{2,6},{3,7},{4,0},{5,1},{6,2},{7,3},{8,12},{9,13},{10,... | collective-permute-start | bytes 196616 | tf_op jit(solution)/shard_map/ppermute | solution.py:363
  97.6 3.3 %collective-permute-done.23.back_last = f32[128,128]{1,0:T(8,128)S(1)} collective-permute-done((f32[128,128]{1,0:T(8,128)S(1)}, f32[128,128]{1,0:T(8,128)S(1)}, u32[]{:S(2)}, u32[]{:S(2)}) %collective-permute-start.23) | collective-permute-done | bytes 65568 | tf_op jit(solution)/shard_map/ppermute | solution.py:363
  101.2 2.1 %own.5.partial_ref = f32[32,4096]{1,0:T(8,128)S(1)} custom-call(f32[32,1024]{1,0:T(8,128)S(1)} %get-tuple-element.72.clipped_ref, bf16[2048,4096]{1,0:T(8,128)(2,1)S(1)} %get-tuple-element.53.high_ref, f8e4m3fn[2048,4096]{1,0:T(32,128)(4,1)S(1)} %get-tuple-element.54.low_ref), custom_call_target="tpu_custom_call" | custom-call | tf_op jit(solution)/shard_map/own/pallas_call | solution.py:331
  104.0 5.6 %rest.5 = (f32[32,4096]{1,0:T(8,128)S(1)}, bf16[64,4096]{1,0:T(8,128)(2,1)S(1)}, f8e4m3fn[32,4096]{1,0:T(32,128)(4,1)S(1)}, f32[264,128]{1,0:T(8,128)S(1)}, f32[40,128]{1,0:T(8,128)S(1)}) custom-call(f32[32,1024]{1,0:T(8,128)S(1)} %collective-permute-done.24.clipped_ref, bf16[2048,4096]{1,0:T(8,128)(2,1)S(1)} %get-tuple-element.53.high_ref, ...), custom_call_target="tpu_custom_call" | custom-call | tf_op jit(solution)/shard_map/rest/pallas_call | solution.py:331
  110.3 3.4 %image.5.own_ref = f32[264,128]{1,0:T(8,128)S(1)} custom-call(bf16[64,4096]{1,0:T(8,128)(2,1)S(1)} %get-tuple-element.73.pair_ref, f8e4m3fn[32,4096]{1,0:T(32,128)(4,1)S(1)} %get-tuple-element.74.coarse_ref, f32[40,128]{1,0:T(8,128)S(1)} %get-tuple-element.75.notes_ref, bf16[2048,4096]{1,0:T(8,128)(2,1)S(1)} %get-tuple-element.53.high_ref, ...), custom_call_target="tpu_custom_call" | custom-call | tf_op jit(solution)/shard_map/image/pallas_call | solution.py:331
  118.1 2.0 %collective-permute-start.27 = (f32[136,128]{1,0:T(8,128)S(1)}, f32[136,128]{1,0:T(8,128)S(1)}, u32[]{:S(2)}, u32[]{:S(2)}) collective-permute-start(f32[136,128]{1,0:T(8,128)S(1)} %add.28.one_ref), channel_id=1, source_target_pairs={{0,2},{1,3},{2,0},{3,1},{4,6},{5,7},{6,4},{7,5},{8,10},{9,11},{10,... | collective-permute-start | bytes 208904 | tf_op jit(solution)/shard_map/ppermute | solution.py:363
  122.5 2.0 %collective-permute-start.28 = (f32[136,128]{1,0:T(8,128)S(1)}, f32[136,128]{1,0:T(8,128)S(1)}, u32[]{:S(2)}, u32[]{:S(2)}) collective-permute-start(f32[136,128]{1,0:T(8,128)S(1)} %add.29.front), channel_id=1, source_target_pairs={{0,4},{1,5},{2,6},{3,7},{4,0},{5,1},{6,2},{7,3},{8,12},{9,13},{10,... | collective-permute-start | bytes 208904 | tf_op jit(solution)/shard_map/ppermute | solution.py:363
  126.1 2.0 %collective-permute-done.28.front_last = f32[136,128]{1,0:T(8,128)S(1)} collective-permute-done((f32[136,128]{1,0:T(8,128)S(1)}, f32[136,128]{1,0:T(8,128)S(1)}, u32[]{:S(2)}, u32[]{:S(2)}) %collective-permute-start.28) | collective-permute-done | bytes 69664 | tf_op jit(solution)/shard_map/ppermute | solution.py:363
  (79 shorter events, 27.5 us)
Async XLA Ops:
  0.6 2.7 %collective-permute-start = (s32[1024,128]{1,0:T(8,128)}, s32[1024,128]{1,0:T(8,128)S(1)}, u32[]{:S(2)}, u32[]{:S(2)}) collective-permute-start(s32[1024,128]{1,0:T(8,128)} %own_ref.1), channel_id=1, source_target_pairs={{0,8},{8,0},{1,9},{9,1},{2,10},{10,2},{3,11},{11,3},{4,12},{12,4},... | collective-permute-start | bytes 1572872 | tf_op jit(solution)/shard_map/ppermute | solution.py:353
  26.9 5.3 %collective-permute-start.2 = (f32[128,128]{1,0:T(8,128)S(1)}, f32[128,128]{1,0:T(8,128)S(1)}, u32[]{:S(2)}, u32[]{:S(2)}) collective-permute-start(f32[128,128]{1,0:T(8,128)S(1)} %get-tuple-element.50.one_ref), channel_id=1, source_target_pairs={{0,1},{1,0},{2,3},{3,2},{4,5},{5,4},{6,7},{7,6},{8,9},{9,8},{10,11... | collective-permute-start | bytes 196616 | tf_op jit(solution)/shard_map/ppermute | solution.py:363
  29.6 4.5 %collective-permute-start.5 = (f32[128,128]{1,0:T(8,128)S(1)}, f32[128,128]{1,0:T(8,128)S(1)}, u32[]{:S(2)}, u32[]{:S(2)}) collective-permute-start(f32[128,128]{1,0:T(8,128)S(1)} %get-tuple-element.51.one_ref), channel_id=1, source_target_pairs={{0,2},{1,3},{2,0},{3,1},{4,6},{5,7},{6,4},{7,5},{8,10},{9,11},{10,... | collective-permute-start | bytes 196616 | tf_op jit(solution)/shard_map/ppermute | solution.py:363
  32.3 4.3 %collective-permute-start.3 = (f32[128,128]{1,0:T(8,128)S(1)}, f32[128,128]{1,0:T(8,128)S(1)}, u32[]{:S(2)}, u32[]{:S(2)}) collective-permute-start(f32[128,128]{1,0:T(8,128)S(1)} %add.16.one_ref), channel_id=1, source_target_pairs={{0,2},{1,3},{2,0},{3,1},{4,6},{5,7},{6,4},{7,5},{8,10},{9,11},{10,... | collective-permute-start | bytes 196616 | tf_op jit(solution)/shard_map/ppermute | solution.py:363
  34.1 5.3 %collective-permute-start.6 = (f32[128,128]{1,0:T(8,128)S(1)}, f32[128,128]{1,0:T(8,128)S(1)}, u32[]{:S(2)}, u32[]{:S(2)}) collective-permute-start(f32[128,128]{1,0:T(8,128)S(1)} %add.18.one_ref), channel_id=1, source_target_pairs={{0,1},{1,0},{2,3},{3,2},{4,5},{5,4},{6,7},{7,6},{8,9},{9,8},{10,11... | collective-permute-start | bytes 196616 | tf_op jit(solution)/shard_map/ppermute | solution.py:363
  36.6 7.3 %collective-permute-start.4 = (f32[128,128]{1,0:T(8,128)S(1)}, f32[128,128]{1,0:T(8,128)S(1)}, u32[]{:S(2)}, u32[]{:S(2)}) collective-permute-start(f32[128,128]{1,0:T(8,128)S(1)} %add.17.front), channel_id=1, source_target_pairs={{0,4},{1,5},{2,6},{3,7},{4,0},{5,1},{6,2},{7,3},{8,12},{9,13},{10,... | collective-permute-start | bytes 196616 | tf_op jit(solution)/shard_map/ppermute | solution.py:363
  39.5 5.2 %collective-permute-start.7 = (f32[128,128]{1,0:T(8,128)S(1)}, f32[128,128]{1,0:T(8,128)S(1)}, u32[]{:S(2)}, u32[]{:S(2)}) collective-permute-start(f32[128,128]{1,0:T(8,128)S(1)} %add.19.back), channel_id=1, source_target_pairs={{0,4},{1,5},{2,6},{3,7},{4,0},{5,1},{6,2},{7,3},{8,12},{9,13},{10,... | collective-permute-start | bytes 196616 | tf_op jit(solution)/shard_map/ppermute | solution.py:363
  44.8 2.2 %collective-permute-start.8 = (f32[32,1024]{1,0:T(8,128)S(1)}, f32[32,1024]{1,0:T(8,128)S(1)}, u32[]{:S(2)}, u32[]{:S(2)}) collective-permute-start(f32[32,1024]{1,0:T(8,128)S(1)} %get-tuple-element.52.clipped_ref), channel_id=1, source_target_pairs={{0,8},{8,0},{1,9},{9,1},{2,10},{10,2},{3,11},{11,3},{4,12},{12,4},... | collective-permute-start | bytes 393224 | tf_op jit(solution)/shard_map/ppermute | solution.py:353
  52.6 4.0 %collective-permute-start.9 = (f32[264,128]{1,0:T(8,128)S(1)}, f32[264,128]{1,0:T(8,128)S(1)}, u32[]{:S(2)}, u32[]{:S(2)}) collective-permute-start(f32[264,128]{1,0:T(8,128)S(1)} %get-tuple-element.59), channel_id=1, source_target_pairs={{0,8},{8,0},{1,9},{9,1},{2,10},{10,2},{3,11},{11,3},{4,12},{12,4},... | collective-permute-start | bytes 405512 | tf_op jit(solution)/shard_map/ppermute | solution.py:353
  56.7 4.4 %collective-permute-start.10 = (f32[136,128]{1,0:T(8,128)S(1)}, f32[136,128]{1,0:T(8,128)S(1)}, u32[]{:S(2)}, u32[]{:S(2)}) collective-permute-start(f32[136,128]{1,0:T(8,128)S(1)} %get-tuple-element.60.one_ref), channel_id=1, source_target_pairs={{0,1},{1,0},{2,3},{3,2},{4,5},{5,4},{6,7},{7,6},{8,9},{9,8},{10,11... | collective-permute-start | bytes 208904 | tf_op jit(solution)/shard_map/ppermute | solution.py:363
  58.2 4.4 %collective-permute-start.13 = (f32[128,128]{1,0:T(8,128)S(1)}, f32[128,128]{1,0:T(8,128)S(1)}, u32[]{:S(2)}, u32[]{:S(2)}) collective-permute-start(f32[128,128]{1,0:T(8,128)S(1)} %get-tuple-element.61.one_ref), channel_id=1, source_target_pairs={{0,2},{1,3},{2,0},{3,1},{4,6},{5,7},{6,4},{7,5},{8,10},{9,11},{10,... | collective-permute-start | bytes 196616 | tf_op jit(solution)/shard_map/ppermute | solution.py:363
  61.0 4.4 %collective-permute-start.11 = (f32[136,128]{1,0:T(8,128)S(1)}, f32[136,128]{1,0:T(8,128)S(1)}, u32[]{:S(2)}, u32[]{:S(2)}) collective-permute-start(f32[136,128]{1,0:T(8,128)S(1)} %add.20.one_ref), channel_id=1, source_target_pairs={{0,2},{1,3},{2,0},{3,1},{4,6},{5,7},{6,4},{7,5},{8,10},{9,11},{10,... | collective-permute-start | bytes 208904 | tf_op jit(solution)/shard_map/ppermute | solution.py:363
  62.7 4.5 %collective-permute-start.14 = (f32[128,128]{1,0:T(8,128)S(1)}, f32[128,128]{1,0:T(8,128)S(1)}, u32[]{:S(2)}, u32[]{:S(2)}) collective-permute-start(f32[128,128]{1,0:T(8,128)S(1)} %add.22.one_ref), channel_id=1, source_target_pairs={{0,1},{1,0},{2,3},{3,2},{4,5},{5,4},{6,7},{7,6},{8,9},{9,8},{10,11... | collective-permute-start | bytes 196616 | tf_op jit(solution)/shard_map/ppermute | solution.py:363
  65.4 7.1 %collective-permute-start.12 = (f32[136,128]{1,0:T(8,128)S(1)}, f32[136,128]{1,0:T(8,128)S(1)}, u32[]{:S(2)}, u32[]{:S(2)}) collective-permute-start(f32[136,128]{1,0:T(8,128)S(1)} %add.21.front), channel_id=1, source_target_pairs={{0,4},{1,5},{2,6},{3,7},{4,0},{5,1},{6,2},{7,3},{8,12},{9,13},{10,... | collective-permute-start | bytes 208904 | tf_op jit(solution)/shard_map/ppermute | solution.py:363
  67.2 5.3 %collective-permute-start.15 = (f32[128,128]{1,0:T(8,128)S(1)}, f32[128,128]{1,0:T(8,128)S(1)}, u32[]{:S(2)}, u32[]{:S(2)}) collective-permute-start(f32[128,128]{1,0:T(8,128)S(1)} %add.23.back), channel_id=1, source_target_pairs={{0,4},{1,5},{2,6},{3,7},{4,0},{5,1},{6,2},{7,3},{8,12},{9,13},{10,... | collective-permute-start | bytes 196616 | tf_op jit(solution)/shard_map/ppermute | solution.py:363
  80.8 4.0 %collective-permute-start.17 = (f32[264,128]{1,0:T(8,128)S(1)}, f32[264,128]{1,0:T(8,128)S(1)}, u32[]{:S(2)}, u32[]{:S(2)}) collective-permute-start(f32[264,128]{1,0:T(8,128)S(1)} %get-tuple-element.67), channel_id=1, source_target_pairs={{0,8},{8,0},{1,9},{9,1},{2,10},{10,2},{3,11},{11,3},{4,12},{12,4},... | collective-permute-start | bytes 405512 | tf_op jit(solution)/shard_map/ppermute | solution.py:353
  84.8 4.4 %collective-permute-start.18 = (f32[136,128]{1,0:T(8,128)S(1)}, f32[136,128]{1,0:T(8,128)S(1)}, u32[]{:S(2)}, u32[]{:S(2)}) collective-permute-start(f32[136,128]{1,0:T(8,128)S(1)} %get-tuple-element.68.one_ref), channel_id=1, source_target_pairs={{0,1},{1,0},{2,3},{3,2},{4,5},{5,4},{6,7},{7,6},{8,9},{9,8},{10,11... | collective-permute-start | bytes 208904 | tf_op jit(solution)/shard_map/ppermute | solution.py:363
  86.4 4.8 %collective-permute-start.21 = (f32[128,128]{1,0:T(8,128)S(1)}, f32[128,128]{1,0:T(8,128)S(1)}, u32[]{:S(2)}, u32[]{:S(2)}) collective-permute-start(f32[128,128]{1,0:T(8,128)S(1)} %get-tuple-element.69.one_ref), channel_id=1, source_target_pairs={{0,2},{1,3},{2,0},{3,1},{4,6},{5,7},{6,4},{7,5},{8,10},{9,11},{10,... | collective-permute-start | bytes 196616 | tf_op jit(solution)/shard_map/ppermute | solution.py:363
  89.2 4.4 %collective-permute-start.19 = (f32[136,128]{1,0:T(8,128)S(1)}, f32[136,128]{1,0:T(8,128)S(1)}, u32[]{:S(2)}, u32[]{:S(2)}) collective-permute-start(f32[136,128]{1,0:T(8,128)S(1)} %add.24.one_ref), channel_id=1, source_target_pairs={{0,2},{1,3},{2,0},{3,1},{4,6},{5,7},{6,4},{7,5},{8,10},{9,11},{10,... | collective-permute-start | bytes 208904 | tf_op jit(solution)/shard_map/ppermute | solution.py:363
  91.2 4.4 %collective-permute-start.22 = (f32[128,128]{1,0:T(8,128)S(1)}, f32[128,128]{1,0:T(8,128)S(1)}, u32[]{:S(2)}, u32[]{:S(2)}) collective-permute-start(f32[128,128]{1,0:T(8,128)S(1)} %add.26.one_ref), channel_id=1, source_target_pairs={{0,1},{1,0},{2,3},{3,2},{4,5},{5,4},{6,7},{7,6},{8,9},{9,8},{10,11... | collective-permute-start | bytes 196616 | tf_op jit(solution)/shard_map/ppermute | solution.py:363
  93.6 7.4 %collective-permute-start.20 = (f32[136,128]{1,0:T(8,128)S(1)}, f32[136,128]{1,0:T(8,128)S(1)}, u32[]{:S(2)}, u32[]{:S(2)}) collective-permute-start(f32[136,128]{1,0:T(8,128)S(1)} %add.25.front), channel_id=1, source_target_pairs={{0,4},{1,5},{2,6},{3,7},{4,0},{5,1},{6,2},{7,3},{8,12},{9,13},{10,... | collective-permute-start | bytes 208904 | tf_op jit(solution)/shard_map/ppermute | solution.py:363
  95.6 5.3 %collective-permute-start.23 = (f32[128,128]{1,0:T(8,128)S(1)}, f32[128,128]{1,0:T(8,128)S(1)}, u32[]{:S(2)}, u32[]{:S(2)}) collective-permute-start(f32[128,128]{1,0:T(8,128)S(1)} %add.27.back), channel_id=1, source_target_pairs={{0,4},{1,5},{2,6},{3,7},{4,0},{5,1},{6,2},{7,3},{8,12},{9,13},{10,... | collective-permute-start | bytes 196616 | tf_op jit(solution)/shard_map/ppermute | solution.py:363
  101.1 2.9 %collective-permute-start.24 = (f32[32,1024]{1,0:T(8,128)S(1)}, f32[32,1024]{1,0:T(8,128)S(1)}, u32[]{:S(2)}, u32[]{:S(2)}) collective-permute-start(f32[32,1024]{1,0:T(8,128)S(1)} %get-tuple-element.72.clipped_ref), channel_id=1, source_target_pairs={{0,8},{8,0},{1,9},{9,1},{2,10},{10,2},{3,11},{11,3},{4,12},{12,4},... | collective-permute-start | bytes 393224 | tf_op jit(solution)/shard_map/ppermute | solution.py:353
  103.5 24.6 %collective-permute-start.29 = (f32[32,4096]{1,0:T(8,128)S(1)}, f32[32,4096]{1,0:T(8,128)S(1)}, u32[]{:S(2)}, u32[]{:S(2)}) collective-permute-start(f32[32,4096]{1,0:T(8,128)S(1)} %sum.1.refs_1_), channel_id=1, source_target_pairs={{0,8},{8,0},{1,9},{9,1},{2,10},{10,2},{3,11},{11,3},{4,12},{12,4},... | collective-permute-start | bytes 1572872 | tf_op jit(solution)/shard_map/ppermute | solution.py:353
  109.7 18.4 %collective-permute-start.30 = (f32[32,4096]{1,0:T(8,128)S(1)}, f32[32,4096]{1,0:T(8,128)S(1)}, u32[]{:S(2)}, u32[]{:S(2)}) collective-permute-start(f32[32,4096]{1,0:T(8,128)S(1)} %get-tuple-element.82.refs_3_), channel_id=1, source_target_pairs={{0,8},{8,0},{1,9},{9,1},{2,10},{10,2},{3,11},{11,3},{4,12},{12,4},... | collective-permute-start | bytes 1572872 | tf_op jit(solution)/shard_map/ppermute | solution.py:353
  109.8 3.9 %collective-permute-start.25 = (f32[264,128]{1,0:T(8,128)S(1)}, f32[264,128]{1,0:T(8,128)S(1)}, u32[]{:S(2)}, u32[]{:S(2)}) collective-permute-start(f32[264,128]{1,0:T(8,128)S(1)} %get-tuple-element.76), channel_id=1, source_target_pairs={{0,8},{8,0},{1,9},{9,1},{2,10},{10,2},{3,11},{11,3},{4,12},{12,4},... | collective-permute-start | bytes 405512 | tf_op jit(solution)/shard_map/ppermute | solution.py:353
  113.7 4.4 %collective-permute-start.26 = (f32[136,128]{1,0:T(8,128)S(1)}, f32[136,128]{1,0:T(8,128)S(1)}, u32[]{:S(2)}, u32[]{:S(2)}) collective-permute-start(f32[136,128]{1,0:T(8,128)S(1)} %get-tuple-element.77.one_ref), channel_id=1, source_target_pairs={{0,1},{1,0},{2,3},{3,2},{4,5},{5,4},{6,7},{7,6},{8,9},{9,8},{10,11... | collective-permute-start | bytes 208904 | tf_op jit(solution)/shard_map/ppermute | solution.py:363
  115.3 4.8 %collective-permute-start.31 = (f32[128,128]{1,0:T(8,128)S(1)}, f32[128,128]{1,0:T(8,128)S(1)}, u32[]{:S(2)}, u32[]{:S(2)}) collective-permute-start(f32[128,128]{1,0:T(8,128)S(1)} %get-tuple-element.84.one_ref), channel_id=1, source_target_pairs={{0,2},{1,3},{2,0},{3,1},{4,6},{5,7},{6,4},{7,5},{8,10},{9,11},{10,... | collective-permute-start | bytes 196616 | tf_op jit(solution)/shard_map/ppermute | solution.py:363
  118.1 4.4 %collective-permute-start.27 = (f32[136,128]{1,0:T(8,128)S(1)}, f32[136,128]{1,0:T(8,128)S(1)}, u32[]{:S(2)}, u32[]{:S(2)}) collective-permute-start(f32[136,128]{1,0:T(8,128)S(1)} %add.28.one_ref), channel_id=1, source_target_pairs={{0,2},{1,3},{2,0},{3,1},{4,6},{5,7},{6,4},{7,5},{8,10},{9,11},{10,... | collective-permute-start | bytes 208904 | tf_op jit(solution)/shard_map/ppermute | solution.py:363
  120.1 4.4 %collective-permute-start.32 = (f32[128,128]{1,0:T(8,128)S(1)}, f32[128,128]{1,0:T(8,128)S(1)}, u32[]{:S(2)}, u32[]{:S(2)}) collective-permute-start(f32[128,128]{1,0:T(8,128)S(1)} %add.30.one_ref), channel_id=1, source_target_pairs={{0,1},{1,0},{2,3},{3,2},{4,5},{5,4},{6,7},{7,6},{8,9},{9,8},{10,11... | collective-permute-start | bytes 196616 | tf_op jit(solution)/shard_map/ppermute | solution.py:363
  122.5 5.6 %collective-permute-start.28 = (f32[136,128]{1,0:T(8,128)S(1)}, f32[136,128]{1,0:T(8,128)S(1)}, u32[]{:S(2)}, u32[]{:S(2)}) collective-permute-start(f32[136,128]{1,0:T(8,128)S(1)} %add.29.front), channel_id=1, source_target_pairs={{0,4},{1,5},{2,6},{3,7},{4,0},{5,1},{6,2},{7,3},{8,12},{9,13},{10,... | collective-permute-start | bytes 208904 | tf_op jit(solution)/shard_map/ppermute | solution.py:363
  124.5 5.3 %collective-permute-start.33 = (f32[128,128]{1,0:T(8,128)S(1)}, f32[128,128]{1,0:T(8,128)S(1)}, u32[]{:S(2)}, u32[]{:S(2)}) collective-permute-start(f32[128,128]{1,0:T(8,128)S(1)} %add.31.back), channel_id=1, source_target_pairs={{0,4},{1,5},{2,6},{3,7},{4,0},{5,1},{6,2},{7,3},{8,12},{9,13},{10,... | collective-permute-start | bytes 196616 | tf_op jit(solution)/shard_map/ppermute | solution.py:363
  (4 other events, 62.8 us)
